TPU v7x, 256 devices: a whole 4x4x8 slice. The times are simulated.
256 devices in a mesh: dp: 64 (over z, x, core), mp: 4 (over y).
Axes of the slice: x: 4, y: 4, z: 8, core: 2. Of those that a mesh axis runs over, the one named last changes fastest.
Arguments:
- view_a: bfloat16 [20480, 4096], P('dp', 'mp'), may hold values from -80 to 80
- view_b: bfloat16 [20480, 4096], P('dp', 'mp'), may hold values from -80 to 80
Outputs:
- grad_a: bfloat16 [20480, 4096], P('dp', 'mp')
- grad_b: bfloat16 [20480, 4096], P('dp', 'mp')
- loss: float32 [], replicated
All inputs are finite; a program needn't handle non-finite values.
Results may differ from a plain program's by a relative error of at most 0.0035.
The roundings to bfloat16 on the way count: a program that leaves them out, or rounds other values in their place, can miss the bound.
Values may be sent and summed in bfloat16 or wider, within the bound.
A program may use at most 64 MiB of HBM per device.

v0:
```python
import jax
import jax.numpy as jnp
from jax import lax
from jax.sharding import PartitionSpec as P

epsilon = 1e-05
off_weight = 0.0051


def per_device(view_a, view_b):
    frames_here = view_a.shape[0]
    width_here = view_a.shape[1]
    members = lax.axis_size("dp")
    total_frames = frames_here * members
    values_a = view_a.astype(jnp.float32)
    values_b = view_b.astype(jnp.float32)
    sum_a, sum_b = lax.psum((jnp.sum(values_a, axis=0), jnp.sum(values_b, axis=0)), "dp")
    center_a = sum_a / total_frames
    center_b = sum_b / total_frames
    dev_a = values_a - center_a
    dev_b = values_b - center_b
    square_a, square_b = lax.psum(
        (jnp.sum(dev_a * dev_a, axis=0), jnp.sum(dev_b * dev_b, axis=0)), "dp"
    )
    spread_a = square_a / total_frames
    spread_b = square_b / total_frames
    inv_a = lax.rsqrt(spread_a + epsilon)
    inv_b = lax.rsqrt(spread_b + epsilon)
    normed_a = (values_a - center_a) * inv_a
    normed_b = (values_b - center_b) * inv_b
    normed_a16 = normed_a.astype(jnp.bfloat16)
    normed_b16 = normed_b.astype(jnp.bfloat16)
    full_b = lax.all_gather(normed_b16, "mp", axis=1, tiled=True)
    width = full_b.shape[1]
    group = lax.axis_index("mp")
    member = lax.axis_index("dp")
    tile_cols = width // members
    partial_value = lax.dot_general(
        normed_a16, full_b, (((0,), (0,)), ((), ())), preferred_element_type=jnp.float32
    )
    corr = lax.psum_scatter(partial_value, "dp", scatter_dimension=1, tiled=True) / total_frames
    row_ids = group * width_here + jnp.arange(width_here, dtype=jnp.int32)
    col_ids = member * tile_cols + jnp.arange(tile_cols, dtype=jnp.int32)
    diagonal = row_ids[:, None] == col_ids[None, :]
    loss_here = jnp.sum(jnp.where(diagonal, (1.0 - corr) ** 2, off_weight * corr * corr))
    slope16 = jnp.where(diagonal, -2.0 * (1.0 - corr), 2.0 * off_weight * corr).astype(jnp.bfloat16)
    slope_slice = lax.all_gather(slope16, "dp", axis=1, tiled=True)
    back_a = lax.dot_general(
        full_b, slope_slice, (((1,), (1,)), ((), ())), preferred_element_type=jnp.float32
    )
    partial_b = jnp.dot(normed_a16, slope_slice, preferred_element_type=jnp.float32)
    back_b = lax.psum_scatter(partial_b, "mp", scatter_dimension=1, tiled=True)
    mean_a, inner_a, mean_b, inner_b = lax.psum(
        (
            jnp.sum(back_a, axis=0),
            jnp.sum(back_a * normed_a, axis=0),
            jnp.sum(back_b, axis=0),
            jnp.sum(back_b * normed_b, axis=0),
        ),
        "dp",
    )
    grad_a = (
        inv_a * (back_a - mean_a / total_frames - normed_a * (inner_a / total_frames))
    ).astype(jnp.bfloat16)
    grad_b = (
        inv_b * (back_b - mean_b / total_frames - normed_b * (inner_b / total_frames))
    ).astype(jnp.bfloat16)
    loss = lax.psum(loss_here, ("dp", "mp"))
    return (grad_a, grad_b, loss)


def solution(mesh):
    placed = (P("dp", "mp"), P("dp", "mp"))
    return jax.shard_map(
        per_device,
        mesh=mesh,
        in_specs=placed,
        out_specs=(P("dp", "mp"), P("dp", "mp"), P()),
        check_vma=False,
    )
```

profile of v0, /device:TPU:1, one launch (start us, length us, event | category | flops | bytes accessed | tf_op | source)
XLA Modules:
  0.0 935.6 jit_solution(10241073266447791041)
XLA Ops:
  7.2 0.0 copy-start
  7.2 0.0 copy-start.1
  7.2 0.0 all-gather.3.cloned.1.call-start
  7.2 1.3 convert_reduce_fusion
  8.5 1.2 convert_reduce_fusion.1
  9.7 130.0 %all-reduce.2 = (f32[1024]{0:T(1024)S(1)}, f32[1024]{0:T(1024)S(1)}) all-reduce(f32[1024]{0:T(1024)S(1)} %convert_reduce_fusion, f32[1024]{0:T(1024)S(1)} %convert_reduce_fusion.1), channel_id=1, replica_groups=mesh['dp'=64,'mp'=4] {'dp'}, use_global_device_ids=true, to_apply=%region_5.0 | all-reduce | flops 2048 | bytes 16384 | tf_op jit(solution)/shard_map/psum | solution.py:17
  139.8 0.0 copy-done.1
  139.8 0.2 fusion.19
  140.0 0.0 copy-done
  140.0 0.2 fusion.14
  140.2 130.5 %all-reduce.1 = (f32[1024]{0:T(1024)S(1)}, f32[1024]{0:T(1024)S(1)}) all-reduce(f32[1024]{0:T(1024)S(1)} %fusion.14, f32[1024]{0:T(1024)S(1)} %fusion.19), channel_id=1, replica_groups=mesh['dp'=64,'mp'=4] {'dp'}, use_global_device_ids=true, to_apply=%region_7.0 | all-reduce | flops 2048 | bytes 16384 | tf_op jit(solution)/shard_map/psum | solution.py:22
  270.7 1.0 fusion.9
  271.7 0.0 all-gather.3.cloned.1.call-update
  271.7 0.0 reduce-scatter.3.cloned.1.call-start
  271.8 32.6 %all-gather.3.cloned.1.call-done = bf16[320,4096]{1,0:T(8,128)(2,1)} async-done(((bf16[320,1024]{1,0:T(8,128)(2,1)}), bf16[320,4096]{1,0:T(8,128)(2,1)}) %all-gather.3.cloned.1.call-update) | async-done | bytes 2621456 | tf_op jit(solution)/shard_map/all_gather | solution.py:33
  304.4 9.9 %fusion.22 = f32[1024,4096]{0,1:T(8,128)} fusion(bf16[320,4096]{1,0:T(8,128)(2,1)} %all-gather.3.cloned.1.call-done, bf16[320,1024]{1,0:T(8,128)(2,1)S(1)} %copy-done.1, f32[1024]{0:T(1024)S(1)} %add_rsqrt_fusion.1, f32[1024]{0:T(1024)S(1)} %get-tuple-element.19), kind=kOutput, calls=%fused_computation.25 | convolution fusion | flops 2685665280 | bytes 20062208 | tf_op jit(solution)/shard_map/dot_general | solution.py:38
  314.4 0.0 reduce-scatter.3.cloned.1.call-update
  314.4 0.0 all-gather.5.cloned.1.call-start
  314.5 185.4 %reduce-scatter.3.cloned.1.call-done = f32[1024,64]{0,1:T(8,128)} async-done(((f32[1024,4096]{0,1:T(8,128)}), f32[1024,64]{0,1:T(8,128)}) %reduce-scatter.3.cloned.1.call-update) | async-done | bytes 262160 | tf_op jit(solution)/shard_map/reduce_scatter | solution.py:41
  499.9 2.4 fusion.25
  502.3 0.0 all-gather.5.cloned.1.call-update
  502.3 0.0 reduce-scatter.5.cloned.1.call-start
  502.3 86.7 %all-gather.5.cloned.1.call-done = bf16[1024,4096]{0,1:T(8,128)(2,1)} async-done(((bf16[1024,64]{0,1:T(8,128)(2,1)}), bf16[1024,4096]{0,1:T(8,128)(2,1)}) %all-gather.5.cloned.1.call-update) | async-done | bytes 8388624 | tf_op jit(solution)/shard_map/all_gather | solution.py:47
  589.1 10.8 %fusion.20 = f32[320,4096]{1,0:T(8,128)} fusion(bf16[1024,4096]{0,1:T(8,128)(2,1)} %all-gather.5.cloned.1.call-done, bf16[320,1024]{1,0:T(8,128)(2,1)S(1)} %copy-done.1, f32[1024]{0:T(1024)S(1)} %add_rsqrt_fusion.1, f32[1024]{0:T(1024)S(1)} %get-tuple-element.19), kind=kOutput, calls=%fused_computation.24 | convolution fusion | flops 2685665280 | bytes 14295040 | tf_op jit(solution)/shard_map/dot_general | solution.py:51
  599.9 0.0 reduce-scatter.5.cloned.1.call-update
  599.9 75.8 %psum.71 = f32[]{:T(128)} all-reduce(f32[]{:T(128)} %get-tuple-element.15), channel_id=1, replica_groups=mesh['dp'=64,'mp'=4] {'dp','mp'}, use_global_device_ids=true, to_apply=%region_19.20 | all-reduce | flops 1 | bytes 8 | tf_op jit(solution)/shard_map/psum | solution.py:68
  675.7 6.1 fusion.27
  681.9 0.0 reduce-scatter.5.cloned.1.call-done
  681.9 1.6 fusion.26
  683.5 242.9 %all-reduce = (f32[1024]{0:T(1024)S(1)}, f32[1024]{0:T(1024)S(1)}, f32[1024]{0:T(1024)S(1)}, f32[1024]{0:T(1024)S(1)}) all-reduce(f32[1024]{0:T(1024)S(1)} %get-tuple-element.6, f32[1024]{0:T(1024)S(1)} %get-tuple-element.5, f32[1024]{0:T(1024)S(1)} %get-tuple-element.4, ...), channel_id=1, replica_groups=mesh['dp'=64,'mp'=4] {'dp'}, use_global_device_ids=true, to_apply=%region_12.13 | all-reduce | flops 4096 | bytes 32768 | tf_op jit(solution)/shard_map/psum | solution.py:53
  926.5 0.0 copy-start.2
  926.5 1.2 fusion.18
  927.6 0.2 copy-done.2
  927.9 1.2 fusion.13
  (9 shorter events, 0.0 us)
Async XLA Ops:
  7.2 132.8 %copy-start = (bf16[320,1024]{1,0:T(8,128)(2,1)S(1)}, bf16[320,1024]{1,0:T(8,128)(2,1)}, u32[]{:S(2)}) copy-start(bf16[320,1024]{1,0:T(8,128)(2,1)} %param.3) | copy-start | bytes 1966084
  7.2 132.6 %copy-start.1 = (bf16[320,1024]{1,0:T(8,128)(2,1)S(1)}, bf16[320,1024]{1,0:T(8,128)(2,1)}, u32[]{:S(2)}) copy-start(bf16[320,1024]{1,0:T(8,128)(2,1)} %param.2) | copy-start | bytes 1966084
  7.2 297.3 %all-gather.3.cloned.1.call-start = ((), (), s32[]{:S(2)}) async-start(), calls=%async_computation.2 | async-start | bytes 3276800 | tf_op jit(solution)/shard_map/all_gather | solution.py:33
  271.7 228.2 %reduce-scatter.3.cloned.1.call-start = ((), (), s32[]{:S(2)}) async-start(), calls=%async_computation.3 | async-start | bytes 17039360 | tf_op jit(solution)/shard_map/reduce_scatter | solution.py:41
  314.4 274.7 %all-gather.5.cloned.1.call-start = ((), (), s32[]{:S(2)}) async-start(), calls=%async_computation.4 | async-start | bytes 8519680 | tf_op jit(solution)/shard_map/all_gather | solution.py:47
  502.3 179.6 %reduce-scatter.5.cloned.1.call-start = ((), (), s32[]{:S(2)}) async-start(), calls=%async_computation.5 | async-start | bytes 6553600 | tf_op jit(solution)/shard_map/reduce_scatter | solution.py:52
  926.5 1.4 copy-start.2
Sparse Core Ops, SparseCore 0:
  271.8 32.5 all-gather.2
  314.5 185.3 reduce-scatter.2
  503.3 85.7 all-gather.4
  600.0 55.6 reduce-scatter.4
where the time goes:
time: 938 us; the launch traced here: 936 us
  blocking collectives  579 us (62%)
  waiting for transfers between devices  305 us (33%)
  matrix products  26.9 us (3%)
  between operations  13.9 us (1%)
  other arithmetic  10.3 us (1%)
    psum x1, blocking collectives, per_device(): lax.psum((jnp.sum(back_a, axis=0), jnp.sum(back_a * normed_a, axis=0), jn...  243 us
    reduce_scatter x1, waiting for transfers between devices, per_device(): lax.psum_scatter(partial_value, 'dp', scatter_dimension=1, tiled=True)  185 us
    psum x1, blocking collectives, per_device(): lax.psum((jnp.sum(dev_a * dev_a, axis=0), jnp.sum(dev_b * dev_b, axis=0))...  130 us
    psum x1, blocking collectives, per_device(): lax.psum((jnp.sum(values_a, axis=0), jnp.sum(values_b, axis=0)), 'dp')  130 us
    all_gather x1, waiting for transfers between devices, per_device(): slope_slice = lax.all_gather(slope16, 'dp', axis=1, tiled=True)  86.7 us
    psum x1, blocking collectives, per_device(): loss = lax.psum(loss_here, ('dp', 'mp'))  75.8 us
    all_gather x1, waiting for transfers between devices, per_device(): full_b = lax.all_gather(normed_b16, 'mp', axis=1, tiled=True)  32.6 us
  transfers between devices with their start and end apart: 4, of which 3 were waited for; matrix products, arithmetic and copies ran while one was open for 1% of the time, Pallas kernels for 0%

commit v1 on v0

v1 whole, which is shorter than its diff:
```python
import functools

import jax
import jax.numpy as jnp
from jax import lax
from jax.experimental import pallas as pl
from jax.experimental.pallas import tpu as pltpu
from jax.sharding import PartitionSpec as P

epsilon = 1e-05
off_weight = 0.0051

MESH = pl.DeviceIdType.MESH
f32 = jnp.float32
bf16 = jnp.bfloat16

SHIFT = (0, 1, 3, 2)
SLOT = (0, 1, 3, 2)


tiny = 1e-37


def encode(v):
    q = v * v
    q = q * q
    return jnp.where(v < 0.0, -q, q).astype(bf16)


def decode(y):
    y = y.astype(f32)
    q = jnp.abs(y)
    q = q * lax.rsqrt(jnp.maximum(q, tiny))
    q = q * lax.rsqrt(jnp.maximum(q, tiny))
    return jnp.where(y < 0.0, -q, q)


def kernel(
    nx, nz, ny, total,
    a_ref, b_ref, ga_ref, gb_ref, loss_ref,
    na16, nb16, na, nat, nb, part, slope, back_a, part_b, sum_b, full_b,
    stat_c, stat_x, stat_z, diag_c, diag_x, diag_z,
    mean_b16, extra_y, extra_c, extra_a, row_acc,
    rx_p1, rx_m1, rx_p2, rx_m2, rz_p1, rz_m1, rz_p2, rz_m2,
    sx_p1, sx_m1, sx_p2, sx_m2, sz_p1, sz_m1, sz_p2, sz_m2,
    ry_p1, ry_m1, ry_p2, ry_m2, sy_p1, sy_m1, sy_p2, sy_m2, recv_a,
    send_sems, recv_sems,
):
    frames, width = a_ref.shape
    both = 2 * frames
    half = width // 2
    quarter = half // 2
    slots = ny
    dp = lax.axis_index("dp")
    m = lax.axis_index("mp")
    c = lax.rem(dp, 2)
    x = lax.rem(dp // 2, nx)
    z = dp // (2 * nx)

    def device(dc=0, dx=0, dz=0, dy=0):
        there = (lax.rem(z + dz, nz) * nx + lax.rem(x + dx, nx)) * 2
        there = there + (1 - c if dc else c)
        return (there, lax.rem(m + dy, ny))

    partner = device(dc=1)
    peers_x = [device(dx=k) for k in range(1, nx)]
    peers_z = [device(dz=k) for k in range(1, nz)]
    peers_y = [device(dy=k) for k in range(1, ny)]
    everyone = [partner] + peers_x + peers_z + peers_y

    barrier = pltpu.get_barrier_semaphore()
    for peer in everyone:
        pl.semaphore_signal(barrier, inc=1, device_id=peer, device_id_type=MESH)

    started = []

    def send(src, dst, peer):
        at = len(started)
        copy = pltpu.make_async_remote_copy(
            src_ref=src,
            dst_ref=dst,
            send_sem=send_sems.at[at],
            recv_sem=recv_sems.at[at],
            device_id=peer,
            device_id_type=MESH,
        )
        copy.start()
        started.append(copy)
        return copy

    def exchange(buf, mine, peers):
        copies = [send(buf.at[mine], buf.at[mine], peer) for peer in peers]
        for copy in copies:
            copy.wait_recv()

    def column_sum(fn):
        step = 64
        def body(i, acc):
            return acc + jnp.sum(fn(pl.ds(i * step, step)), axis=0, keepdims=True)
        return lax.fori_loop(0, frames // step, body, jnp.zeros((1, width), f32))

    for view, ref in enumerate((a_ref, b_ref)):
        center = column_sum(lambda rows: ref[rows, :].astype(f32)) / frames
        def deviation(rows, ref=ref, center=center):
            dev = ref[rows, :].astype(f32) - center
            return dev * dev
        stat_c[c, 0, view : view + 1, :] = center
        stat_c[c, 1, view : view + 1, :] = column_sum(deviation)

    pl.semaphore_wait(barrier, len(everyone))

    def merge(buf, members, count):
        center = sum(buf[i, 0] for i in range(members)) * (1.0 / members)
        spread = sum(buf[i, 1] for i in range(members))
        shift = sum((buf[i, 0] - center) ** 2 for i in range(members))
        return center, spread + count * shift

    exchange(stat_c, c, [partner])
    stat_x[x, 0], stat_x[x, 1] = merge(stat_c, 2, float(frames))
    exchange(stat_x, x, peers_x)
    stat_z[z, 0], stat_z[z, 1] = merge(stat_x, nx, float(frames * 2))
    exchange(stat_z, z, peers_z)
    center, spread = merge(stat_z, nz, float(frames * 2 * nx))
    inv = lax.rsqrt(spread / total + epsilon)
    center_a, center_b = center[0:1], center[1:2]
    inv_a, inv_b = inv[0:1], inv[1:2]

    def standardize(i, acc):
        step = 64
        rows = pl.ds(pl.multiple_of(i * step, step), step)
        wide_a = (a_ref[rows, :].astype(f32) - center_a) * inv_a
        wide_b = (b_ref[rows, :].astype(f32) - center_b) * inv_b
        short_a, short_b = wide_a.astype(bf16), wide_b.astype(bf16)
        here = pl.ds(pl.multiple_of(c * frames + i * step, step), step)
        na16[rows, :] = short_a
        nb16[rows, :] = short_b
        back_a16, back_b16 = short_a.astype(f32), short_b.astype(f32)
        terms = (back_a16, back_b16, back_a16 * back_b16, wide_a * back_b16, wide_b * back_a16)
        return tuple(s + jnp.sum(t, axis=0, keepdims=True) for s, t in zip(acc, terms))

    sums = lax.fori_loop(0, frames // 64, standardize, (jnp.zeros((1, width), f32),) * 5)
    diag_c[c, 0, 0:1, :] = sums[0]
    diag_c[c, 0, 1:2, :] = sums[1]
    diag_c[c, 1, 0:1, :] = sums[2]
    diag_c[c, 1, 1:2, :] = jnp.zeros((1, width), f32)
    diag_c[c, 2, 0:1, :] = sums[3]
    diag_c[c, 2, 1:2, :] = sums[4]

    own_frames = pl.ds(pl.multiple_of(c * frames, 64), frames)
    other_frames = pl.ds(pl.multiple_of((1 - c) * frames, 64), frames)
    own_half = pl.ds(pl.multiple_of(c * half, 128), half)
    other_half = pl.ds(pl.multiple_of((1 - c) * half, 128), half)
    swap_b = send(nb16.at[:, other_half], nb.at[0, own_frames, :], partner)
    swap_a = send(na16, na.at[own_frames, :], partner)
    na[own_frames, :] = na16[...]
    nb[0, own_frames, :] = nb16[:, own_half]
    swap_b.wait_recv()

    up, down = device(dy=1), device(dy=ny - 1)
    first = [send(nb.at[0], nb.at[2], up), send(nb.at[0], nb.at[1], down)]
    swap_a.wait_recv()
    for i in range(width // 128):
        cols = pl.ds(i * 128, 128)
        nat[cols, :] = jnp.transpose(na[:, cols].astype(f32)).astype(bf16)

    exchange(diag_c, c, [partner])
    diag_x[x] = sum(diag_c[i] for i in range(2))
    exchange(diag_x, x, peers_x)
    diag_z[z] = sum(diag_x[i] for i in range(nx))
    exchange(diag_z, z, peers_z)
    diag = sum(diag_z[i] for i in range(nz)) / total
    mean_a16, mean_own_b16 = diag[0, 0:1], diag[0, 1:2]
    corr_ii = diag[1, 0:1]
    cross_a, cross_b = diag[2, 0:1], diag[2, 1:2]
    slope_ii = (-2.0 * (1.0 - corr_ii)).astype(bf16).astype(f32)

    def pick(row):
        return jnp.where(c == 0, row[:, :half], row[:, half:])

    mean_b16[0] = pick(mean_own_b16)
    share_b = [send(mean_b16.at[0], mean_b16.at[SLOT[ny - k]], peers_y[k - 1]) for k in range(1, ny)]

    for copy in first:
        copy.wait_recv()
    low, high = pl.ds(0, frames), pl.ds(frames, frames)
    second = [
        send(nb.at[2, low], nb.at[3, low], up),
        send(nb.at[1, high], nb.at[3, high], down),
    ]

    def correlate(p):
        def body(i, _):
            rows = pl.ds(pl.multiple_of(i * 256, 256), 256)
            part[p, rows, :] = jnp.dot(
                nat[rows, :], nb[p], preferred_element_type=f32
            )
            return 0
        lax.fori_loop(0, width // 256, body, 0)

    for p in range(3):
        correlate(p)
    for copy in second:
        copy.wait_recv()
    correlate(3)

    left, right = pl.ds(0, quarter), pl.ds(quarter, quarter)
    every = pl.ds(0, half)

    def sweep(group, rows, fn):
        first, count = group
        step = min(rows, 32)
        def body(i, _):
            p = first + i // (rows // step)
            at = lax.rem(i, rows // step) * step
            fn(p, pl.multiple_of(at, 16), step)
            return 0
        lax.fori_loop(0, count * (rows // step), body, 0)

    def reduce_chain(group, base, rows, n, at, plus, minus, off, bufs):
        out_p1, out_m1, out_p2, out_m2, in_p1, in_m1, in_p2, in_m2 = bufs
        far = n // 2
        some = pl.ds(*group)
        window = pl.ds(off, rows)

        def pack(s, source, cols, out1, out2, in1, in2):
            def fn(p, r, step):
                there = pl.ds(pl.multiple_of(source + r, 16), step)
                here = pl.ds(pl.multiple_of(off + r, 16), step)
                if s == 1:
                    out1[p, here, :] = encode(part[p, there, cols])
                    return
                if s > 2:
                    out2[s - 2, p, here, :] = encode(part[p, there, :] + decode(in2[s - 3, p, here, :]))
                    return
                rest = right if cols is left else left
                out2[0, p, here, cols] = encode(part[p, there, cols] + decode(in1[p, here, :]))
                out2[0, p, here, rest] = encode(part[p, there, rest])
            sweep(group, rows, fn)

        for s in range(1, far + 1):
            distance = far + 1 - s
            pack(s, base + lax.rem(at + distance, n) * rows, left, out_p1, out_p2, in_p1, in_p2)
            pack(s, base + lax.rem(at + n - distance, n) * rows, right, out_m1, out_m2, in_m1, in_m2)
            def view(first, later):
                return first.at[some, window] if s == 1 else later.at[s - 2, some, window]
            go = [
                send(view(out_p1, out_p2), view(in_p1, in_p2), plus),
                send(view(out_m1, out_m2), view(in_m1, in_m2), minus),
            ]
            yield
            for copy in go:
                copy.wait_recv()

        def finish(p, r, step):
            there = pl.ds(pl.multiple_of(base + at * rows + r, 16), step)
            here = pl.ds(pl.multiple_of(off + r, 16), step)
            part[p, there, :] += decode(in_p2[far - 2, p, here, :]) + decode(in_m2[far - 2, p, here, :])
        sweep(group, rows, finish)

    def gather_chain(base, rows, n, at, plus, minus):
        far = n // 2
        for s in range(1, far + 1):
            cols_p, cols_m = (left, right) if s == far else (every, every)
            from_p = base + lax.rem(at + n - (s - 1), n) * rows
            from_m = base + lax.rem(at + (s - 1), n) * rows
            there_p = pl.ds(pl.multiple_of(from_p, 16), rows)
            there_m = pl.ds(pl.multiple_of(from_m, 16), rows)
            ref_p = slope.at[:, there_p, cols_p]
            ref_m = slope.at[:, there_m, cols_m]
            go = [send(ref_p, ref_p, plus), send(ref_m, ref_m, minus)]
            yield
            for copy in go:
                copy.wait_recv()

    def in_turn(chains):
        live = list(chains)
        while live:
            for chain in list(live):
                if next(chain, live) is live:
                    live.remove(chain)

    plus_x, minus_x = device(dx=1), device(dx=nx - 1)
    plus_z, minus_z = device(dz=1), device(dz=nz - 1)
    top = width // 2
    rows_x, rows_z, rows_o = top // nx, top // nz, top // (nx * nz)
    base_x = x * rows_x
    base_z = top + z * rows_z

    bufs_x = (sx_p1, sx_m1, sx_p2, sx_m2, rx_p1, rx_m1, rx_p2, rx_m2)
    bufs_z = (sz_p1, sz_m1, sz_p2, sz_m2, rz_p1, rz_m1, rz_p2, rz_m2)

    def one_way(group):
        yield from reduce_chain(group, 0, rows_x, nx, x, plus_x, minus_x, 0, bufs_x)
        yield from reduce_chain(group, base_x, rows_o, nz, z, plus_z, minus_z, rows_z, bufs_z)

    def other_way(group):
        yield from reduce_chain(group, top, rows_z, nz, z, plus_z, minus_z, 0, bufs_z)
        yield from reduce_chain(group, base_z, rows_o, nx, x, plus_x, minus_x, rows_x, bufs_x)

    in_turn([one_way((0, slots)), other_way((0, slots))])

    own_x = base_x + z * rows_o
    own_z = base_z + x * rows_o
    row_ids = lax.broadcasted_iota(jnp.int32, (rows_o, half), 0)
    col_ids = lax.broadcasted_iota(jnp.int32, (rows_o, half), 1)
    for base in (own_x, own_z):
        rows = pl.ds(pl.multiple_of(base, 16), rows_o)
        for p in range(slots):
            corr = part[p, rows, :] / total
            value = 2.0 * off_weight * corr
            if p == 0:
                value = jnp.where(row_ids + base == col_ids + c * half, 0.0, value)
            slope[p, rows, :] = value.astype(bf16)

    def one_way():
        yield from gather_chain(base_x, rows_o, nz, z, plus_z, minus_z)
        yield from gather_chain(0, rows_x, nx, x, plus_x, minus_x)

    def other_way():
        yield from gather_chain(base_z, rows_o, nx, x, plus_x, minus_x)
        yield from gather_chain(top, rows_z, nz, z, plus_z, minus_z)

    in_turn([one_way(), other_way()])
    for copy in share_b:
        copy.wait_recv()

    scale = 1.0 / (2.0 * off_weight)
    row_acc[...] = jnp.zeros_like(row_acc)
    loss_here = jnp.zeros((1, half), f32)
    loss_diag = jnp.sum((1.0 - pick(corr_ii)) ** 2, axis=1, keepdims=True)
    ext_a = jnp.broadcast_to(mean_a16, (16, width)).astype(bf16)
    mean_a = jnp.zeros((16, width), f32)
    inner_b = []
    mean_b = []
    for p in range(slots):
        def body(i, acc, p=p):
            rows = pl.ds(pl.multiple_of(i * 32, 32), 32)
            s = slope[p, rows, :].astype(f32)
            s = s * s
            row_acc[rows, :] += sum(s[:, k * 128 : (k + 1) * 128] for k in range(half // 128))
            return acc + jnp.sum(s, axis=0, keepdims=True)
        square = lax.fori_loop(0, width // 32, body, jnp.zeros((1, half), f32))
        inner_b.append(square * scale)
        loss_here = loss_here + square
        mean_b.append(jnp.dot(ext_a, slope[p], preferred_element_type=f32)[0:1])
        ext_b = jnp.broadcast_to(mean_b16[p], (16, half)).astype(bf16)
        mean_a = mean_a + lax.dot_general(
            ext_b, slope[p], (((1,), (1,)), ((), ())), preferred_element_type=f32)
    loss_off = jnp.sum(loss_here, axis=1, keepdims=True) * (off_weight * scale * scale)
    loss_row = jnp.broadcast_to(loss_off + loss_diag, (1, half))
    for p in range(slots):
        block = extra_y.at[ny + p] if p else extra_y.at[m]
        block[0:1, :] = mean_b[p]
        block[1:2, :] = inner_b[p]
        block[2:3, :] = loss_row
        block[3:4, :] = jnp.zeros((1, half), f32)
    share_y = [
        send(extra_y.at[ny + SLOT[k]], extra_y.at[m], peers_y[k - 1]) for k in range(1, ny)
    ]
    inner_a = jnp.sum(jnp.transpose(row_acc[...]), axis=0, keepdims=True) * scale
    extra_a[c, 0:1, :] = mean_a[0:1]
    extra_a[c, 1:2, :] = inner_a
    share_a = send(extra_a.at[c], extra_a.at[c], partner)

    def back_to_b(p):
        def body(i, _):
            cols = pl.ds(pl.multiple_of(i * 256, 256), 256)
            part_b[p, :, cols] = jnp.dot(
                na[...], slope[p, :, cols], preferred_element_type=f32
            )
            return 0
        lax.fori_loop(0, half // 256, body, 0)

    back_to_b(3)
    def first_y(i, _):
        here = pl.ds(pl.multiple_of(i * 32, 32), 32)
        there = pl.ds(pl.multiple_of(i * 32 + frames, 32), 32)
        sy_p1[here, :] = encode(part_b[3, here, :])
        sy_m1[here, :] = encode(part_b[3, there, :])
        return 0

    lax.fori_loop(0, frames // 32, first_y, 0)
    far = [send(sy_p1, ry_p1, up), send(sy_m1, ry_m1, down)]
    back_to_b(1)
    back_to_b(2)

    def back_to_a(i, _):
        cols = pl.ds(pl.multiple_of(i * 256, 256), 256)
        acc = None
        for p in range(slots):
            term = lax.dot_general(
                nb[p], slope[p, cols, :], (((1,), (1,)), ((), ())), preferred_element_type=f32)
            acc = term if acc is None else acc + term
        back_a[:, cols] = acc
        return 0

    for copy in far:
        copy.wait_recv()

    def second_y(i, _):
        here = pl.ds(pl.multiple_of(i * 32, 32), 32)
        there = pl.ds(pl.multiple_of(i * 32 + frames, 32), 32)
        sy_p2[here, :] = encode(part_b[1, here, :] + decode(ry_p1[here, :]))
        sy_p2[there, :] = encode(part_b[1, there, :])
        sy_m2[here, :] = encode(part_b[2, here, :])
        sy_m2[there, :] = encode(part_b[2, there, :] + decode(ry_m1[here, :]))
        return 0

    lax.fori_loop(0, frames // 32, second_y, 0)
    near = [send(sy_p2, ry_p2, up), send(sy_m2, ry_m2, down)]
    lax.fori_loop(0, width // 256, back_to_a, 0)
    swap_back = send(back_a.at[other_frames, :], recv_a, partner)
    back_to_b(0)
    for copy in near:
        copy.wait_recv()

    def add_last(i, _):
        rows = pl.ds(pl.multiple_of(i * 32, 32), 32)
        sum_b[rows, :] = (
            part_b[0, rows, :] + decode(ry_p2[rows, :]) + decode(ry_m2[rows, :])
        )
        return 0

    lax.fori_loop(0, both // 32, add_last, 0)
    swap_b2 = send(sum_b.at[other_frames, :], full_b.at[:, own_half], partner)
    for copy in share_y:
        copy.wait_recv()
    extra_c[c] = sum(extra_y[i] for i in range(ny))
    share_c = send(extra_c.at[c], extra_c.at[c], partner)
    full_b[:, own_half] = sum_b[own_frames, :]

    share_a.wait_recv()
    last_a = extra_a[0] + extra_a[1]
    mean_a = last_a[0:1] + mean_own_b16 * slope_ii
    inner_a = last_a[1:2] + cross_a * slope_ii
    swap_back.wait_recv()

    def finish_a(i, _):
        rows = pl.ds(pl.multiple_of(i * 32, 32), 32)
        here = pl.ds(pl.multiple_of(c * frames + i * 32, 32), 32)
        wide = (a_ref[rows, :].astype(f32) - center_a) * inv_a
        back = back_a[here, :] + recv_a[rows, :] + slope_ii * nb16[rows, :].astype(f32)
        ga_ref[rows, :] = (inv_a * (back - mean_a - wide * inner_a)).astype(bf16)
        return 0

    lax.fori_loop(0, frames // 32, finish_a, 0)

    share_c.wait_recv()
    mean_b = jnp.concatenate([extra_c[0, 0:1], extra_c[1, 0:1]], axis=1) + mean_a16 * slope_ii
    inner_b = jnp.concatenate([extra_c[0, 1:2], extra_c[1, 1:2]], axis=1) + cross_b * slope_ii
    loss_ref[...] = jnp.broadcast_to(extra_c[0, 2:3, :128] + extra_c[1, 2:3, :128], (8, 128))
    swap_b2.wait_recv()

    def finish_b(i, _):
        rows = pl.ds(pl.multiple_of(i * 32, 32), 32)
        wide = (b_ref[rows, :].astype(f32) - center_b) * inv_b
        back = full_b[rows, :] + slope_ii * na16[rows, :].astype(f32)
        gb_ref[rows, :] = (inv_b * (back - mean_b - wide * inner_b)).astype(bf16)
        return 0

    lax.fori_loop(0, frames // 32, finish_b, 0)
    for copy in started:
        copy.wait_send()


def solution(mesh):
    ny = mesh.shape["mp"]
    members = mesh.shape["dp"]
    nx = ny
    nz = members // (2 * nx)

    def per_device(view_a, view_b):
        frames, width = view_a.shape
        both, half = 2 * frames, width // 2
        quarter = half // 2
        top = width // 2
        rows_x, rows_z, rows_o = top // nx, top // nz, top // (nx * nz)
        vmem = pltpu.VMEM
        rings = []
        scratch = [
            vmem((frames, width), bf16),
            vmem((frames, width), bf16),
            vmem((both, width), bf16),
            vmem((width, both), bf16),
            vmem((ny, both, half), bf16),
            vmem((ny, width, half), f32),
            vmem((ny, width, half), bf16),
            vmem((both, width), f32),
            vmem((ny, both, half), f32),
            vmem((both, half), f32),
            vmem((frames, width), f32),
            vmem((2, 2, 2, width), f32),
            vmem((nx, 2, 2, width), f32),
            vmem((nz, 2, 2, width), f32),
            vmem((2, 3, 2, width), f32),
            vmem((nx, 3, 2, width), f32),
            vmem((nz, 3, 2, width), f32),
            vmem((ny, 1, half), f32),
            vmem((2 * ny, 4, half), f32),
            vmem((2, 4, half), f32),
            vmem((2, 2, width), f32),
            vmem((width, 128), f32),
        ]
        for rows, n in ((rows_x + rows_o, nx), (rows_z + rows_o, nz)):
            ring = [vmem((ny, rows, quarter), bf16)] * 2 + [vmem((n // 2 - 1, ny, rows, half), bf16)] * 2
            rings.append(ring)
        ring_y = [vmem((frames, half), bf16)] * 2 + [vmem((both, half), bf16)] * 2
        scratch += rings[0] + rings[1] + rings[0] + rings[1] + ring_y + ring_y + [
            vmem((frames, width), f32),
            pltpu.SemaphoreType.DMA((110,)),
            pltpu.SemaphoreType.DMA((110,)),
        ]
        grad_a, grad_b, loss = pl.pallas_call(
            functools.partial(kernel, nx, nz, ny, float(frames * members)),
            out_shape=(
                jax.ShapeDtypeStruct((frames, width), bf16),
                jax.ShapeDtypeStruct((frames, width), bf16),
                jax.ShapeDtypeStruct((8, 128), f32),
            ),
            in_specs=[pl.BlockSpec(memory_space=vmem)] * 2,
            out_specs=[pl.BlockSpec(memory_space=vmem)] * 3,
            scratch_shapes=scratch,
            compiler_params=pltpu.CompilerParams(
                collective_id=0, has_side_effects=True, vmem_limit_bytes=56 * 1024 * 1024
            ),
            cost_estimate=pl.CostEstimate(
                flops=3 * 2 * both * width * half * ny, bytes_accessed=4 * frames * width * 2,
                transcendentals=0),
        )(view_a, view_b)
        return grad_a, grad_b, loss[0, 0]

    placed = P("dp", "mp")
    return jax.shard_map(
        per_device,
        mesh=mesh,
        in_specs=(placed, placed),
        out_specs=(placed, placed, P()),
        check_vma=False,
    )
```

time: 938 us -> 174 us (0.19)
  blocking collectives: 579 us -> 0 us
  waiting for transfers between devices: 305 us -> 0 us
  Pallas kernels: 0 us -> 168 us
  matrix products: 26.9 us -> 0 us
  between operations: 13.9 us -> 0.64 us
  other arithmetic: 10.3 us -> 0 us
    psum x4 -> x0, blocking collectives: 579 us -> none  [the longest x1 243 us: per_device(): lax.psum((jnp.sum(back_a, axis=0), jnp.sum(back_a * normed_a, axis=0), jn...]
    reduce_scatter x2 -> x0, waiting for transfers between devices: 185 us -> none  [the longest x1 185 us: per_device(): lax.psum_scatter(partial_value, 'dp', scatter_dimension=1, tiled=True)]
    pallas_call x0 -> x1, Pallas kernels: none -> 168 us  [per_device(): pl.pallas_call(functools.partial(kernel, nx, nz, ny, float(frames * membe...]
    all_gather x2 -> x0, waiting for transfers between devices: 119 us -> none  [the longest x1 86.7 us: per_device(): slope_slice = lax.all_gather(slope16, 'dp', axis=1, tiled=True)]
    dot_general x3 -> x0, matrix products: 26.9 us -> none  [the longest x1 10.8 us: per_device(): jnp.dot(normed_a16, slope_slice, preferred_element_type=jnp.float32)]
  transfers between devices with their start and end apart: 4 -> 0, of which waited for: 3 -> 0; matrix products, arithmetic and copies ran while one was open for 1% -> 0% of each run, Pallas kernels for 0% -> 0%
where the time goes in v1:
time: 174 us; the launch traced here: 172 us
  Pallas kernels  168 us (97%)
  local copies, waits for them, and re-layouts  4.06 us (2%)
    pallas_call x1, Pallas kernels, per_device(): pl.pallas_call(functools.partial(kernel, nx, nz, ny, float(frames * membe...  168 us

profile of v1, /device:TPU:1, one launch (start us, length us, event | category | flops | bytes accessed | tf_op | source)
XLA Modules:
  0.0 172.4 jit_solution(2790465056333638503)
XLA Ops:
  0.6 167.7 %shard_map.49 = (bf16[320,1024]{1,0:T(8,128)(2,1)}, bf16[320,1024]{1,0:T(8,128)(2,1)}, f32[8,128]{1,0:T(8,128)}) custom-call(bf16[320,1024]{1,0:T(8,128)(2,1)} %a_ref.1, bf16[320,1024]{1,0:T(8,128)(2,1)} %b_ref.1), custom_call_target="tpu_custom_call" | custom-call | flops 8053063680 | bytes 2621440 | tf_op jit(solution)/shard_map/pallas_call | solution.py:513
  168.3 1.2 slice.3
  169.5 0.0 copy-start
  169.5 2.0 %copy.7 = bf16[320,1024]{1,0:T(8,128)(2,1)} copy(bf16[320,1024]{1,0:T(8,128)(2,1)} %get-tuple-element.12) | data formatting | bytes 1310720
  171.5 0.0 copy-done
  171.5 0.8 copy.8
Async XLA Ops:
  169.5 2.0 %copy-start = (bf16[320,1024]{1,0:T(8,128)(2,1)S(1)}, bf16[320,1024]{1,0:T(8,128)(2,1)}, u32[]{:S(2)}) copy-start(bf16[320,1024]{1,0:T(8,128)(2,1)} %get-tuple-element.13) | copy-start | bytes 1966084

commit v2 on v1

v2 whole, which is shorter than its diff:
```python
import functools

import jax
import jax.numpy as jnp
from jax import lax
from jax.experimental import pallas as pl
from jax.experimental.pallas import tpu as pltpu
from jax.sharding import PartitionSpec as P

epsilon = 1e-05
off_weight = 0.0051

MESH = pl.DeviceIdType.MESH
f32 = jnp.float32
bf16 = jnp.bfloat16

SHIFT = (0, 1, 3, 2)
SLOT = (0, 1, 3, 2)


tiny = 1e-37


def encode(v):
    q = v * v
    q = q * q
    return jnp.where(v < 0.0, -q, q).astype(bf16)


def decode(y):
    y = y.astype(f32)
    q = jnp.abs(y)
    q = q * lax.rsqrt(jnp.maximum(q, tiny))
    q = q * lax.rsqrt(jnp.maximum(q, tiny))
    return jnp.where(y < 0.0, -q, q)


def kernel(
    nx, nz, ny, total,
    a_ref, b_ref, ga_ref, gb_ref, loss_ref,
    nb16, na, nat, nb, part, slope, back_a, part_b, sum_b, full_b,
    stat_c, stat_x, stat_z, diag_c, diag_x, diag_z, diag_f,
    mean_b16, square, extra_y, extra_c, extra_a, row_acc,
    rx_p1, rx_m1, rx_p2, rx_m2, rz_p1, rz_m1, rz_p2, rz_m2,
    sx_p1, sx_m1, sx_p2, sx_m2, sz_p1, sz_m1, sz_p2, sz_m2,
    ry_p1, ry_m1, ry_p2, ry_m2, sy_p1, sy_m1, sy_p2, sy_m2, recv_a,
    send_sems, recv_sems,
):
    frames, width = a_ref.shape
    both = 2 * frames
    half = width // 2
    slots = ny
    dp = lax.axis_index("dp")
    m = lax.axis_index("mp")
    c = lax.rem(dp, 2)
    x = lax.rem(dp // 2, nx)
    z = dp // (2 * nx)

    def device(dc=0, dx=0, dz=0, dy=0):
        there = (lax.rem(z + dz, nz) * nx + lax.rem(x + dx, nx)) * 2
        there = there + (1 - c if dc else c)
        return (there, lax.rem(m + dy, ny))

    partner = device(dc=1)
    peers_x = [device(dx=k) for k in range(1, nx)]
    peers_z = [device(dz=k) for k in range(1, nz)]
    peers_y = [device(dy=k) for k in range(1, ny)]
    everyone = [partner] + peers_x + peers_z + peers_y

    barrier = pltpu.get_barrier_semaphore()
    for peer in everyone:
        pl.semaphore_signal(barrier, inc=1, device_id=peer, device_id_type=MESH)

    started = []

    def send(src, dst, peer):
        at = len(started)
        copy = pltpu.make_async_remote_copy(
            src_ref=src,
            dst_ref=dst,
            send_sem=send_sems.at[at],
            recv_sem=recv_sems.at[at],
            device_id=peer,
            device_id_type=MESH,
        )
        copy.start()
        started.append(copy)
        return copy

    def arrive(copies):
        for copy in copies:
            copy.wait_recv()

    def spread_to(buf, mine, peers):
        return [send(buf.at[mine], buf.at[mine], peer) for peer in peers]

    def column_sum(fn):
        step = 64
        def body(i, acc):
            return acc + jnp.sum(fn(pl.ds(i * step, step)), axis=0, keepdims=True)
        return lax.fori_loop(0, frames // step, body, jnp.zeros((1, width), f32))

    for view, ref in enumerate((a_ref, b_ref)):
        center = column_sum(lambda rows: ref[rows, :].astype(f32)) / frames
        def deviation(rows, ref=ref, center=center):
            dev = ref[rows, :].astype(f32) - center
            return dev * dev
        stat_c[c, 0, view : view + 1, :] = center
        stat_c[c, 1, view : view + 1, :] = column_sum(deviation)

    pl.semaphore_wait(barrier, len(everyone))

    def merge(buf, members, count):
        center = sum(buf[i, 0] for i in range(members)) * (1.0 / members)
        spread = sum(buf[i, 1] for i in range(members))
        shift = sum((buf[i, 0] - center) ** 2 for i in range(members))
        return center, spread + count * shift

    arrive(spread_to(stat_c, c, [partner]))
    stat_x[x, 0], stat_x[x, 1] = merge(stat_c, 2, float(frames))
    arrive(spread_to(stat_x, x, peers_x))
    stat_z[z, 0], stat_z[z, 1] = merge(stat_x, nx, float(frames * 2))
    arrive(spread_to(stat_z, z, peers_z))
    center, spread = merge(stat_z, nz, float(frames * 2 * nx))
    inv = lax.rsqrt(spread / total + epsilon)
    center_a, center_b = center[0:1], center[1:2]
    inv_a, inv_b = inv[0:1], inv[1:2]

    own, other = pl.ds(0, frames), pl.ds(frames, frames)
    own_half = pl.ds(pl.multiple_of(c * half, 128), half)
    other_half = pl.ds(pl.multiple_of((1 - c) * half, 128), half)

    def standardize(src, dst, center, inv):
        def body(i, _):
            rows = pl.ds(pl.multiple_of(i * 32, 32), 32)
            dst[rows, :] = ((src[rows, :].astype(f32) - center) * inv).astype(bf16)
            return 0
        lax.fori_loop(0, frames // 32, body, 0)

    standardize(b_ref, nb16, center_b, inv_b)
    swap_b = send(nb16.at[:, other_half], nb.at[0, other], partner)
    nb[0, own, :] = nb16[:, own_half]
    up, down = device(dy=1), device(dy=ny - 1)
    first = [send(nb.at[0, own], nb.at[2, own], up)]
    standardize(a_ref, na, center_a, inv_a)
    swap_a = send(na.at[own], na.at[other], partner)
    swap_b.wait_recv()
    first.append(send(nb.at[0, other], nb.at[1, other], down))

    def diagonal():
        def body(i, acc):
            rows = pl.ds(pl.multiple_of(i * 32, 32), 32)
            wide_a = (a_ref[rows, :].astype(f32) - center_a) * inv_a
            wide_b = (b_ref[rows, :].astype(f32) - center_b) * inv_b
            short_a, short_b = na[rows, :].astype(f32), nb16[rows, :].astype(f32)
            terms = (short_a, short_b, short_a * short_b, wide_a * short_b, wide_b * short_a)
            return tuple(s + jnp.sum(t, axis=0, keepdims=True) for s, t in zip(acc, terms))
        sums = lax.fori_loop(0, frames // 32, body, (jnp.zeros((1, width), f32),) * 5)
        for at, value in enumerate(sums[:3] + (jnp.zeros((1, width), f32),) + sums[3:]):
            diag_c[c, at // 2, at % 2 : at % 2 + 1, :] = value
        copies = spread_to(diag_c, c, [partner])
        yield
        arrive(copies)
        diag_x[x] = jnp.where(
            c == 0, diag_c[0, :, :, :half] + diag_c[1, :, :, :half],
            diag_c[0, :, :, half:] + diag_c[1, :, :, half:])
        copies = spread_to(diag_x, x, peers_x)
        yield
        arrive(copies)
        diag_z[z] = sum(diag_x[i] for i in range(nx))
        copies = spread_to(diag_z, z, peers_z)
        yield
        arrive(copies)
        diag_f[c] = sum(diag_z[i] for i in range(nz)) / total
        mean_b16[0] = diag_f[c, 0, 1:2]
        copies = spread_to(diag_f, c, [partner])
        copies += [send(mean_b16.at[0], mean_b16.at[SLOT[ny - k]], peers_y[k - 1]) for k in range(1, ny)]
        yield
        arrive(copies)
        mean_a = jnp.concatenate([diag_f[0, 0, 0:1], diag_f[1, 0, 0:1]], axis=1)
        na[pl.ds(both, 16), :] = jnp.broadcast_to(mean_a, (16, width)).astype(bf16)
        for p in range(slots):
            nb[p, pl.ds(both, 16), :] = jnp.broadcast_to(mean_b16[p], (16, half)).astype(bf16)

    def correlate(p):
        def body(i, _):
            rows = pl.ds(pl.multiple_of(i * 256, 256), 256)
            part[p, rows, :] = jnp.dot(nat[rows, :], nb[p, :both, :], preferred_element_type=f32)
            return 0
        lax.fori_loop(0, width // 256, body, 0)

    def sweep(group, rows, fn):
        first, count, _, columns = group
        step = min(rows, 32)
        turns = count * (rows // step)
        per = min(turns, max(1, 16384 // (step * columns)))
        def body(i, _):
            stores = []
            for u in range(per):
                k = i * per + u
                p = first + k // (rows // step)
                r = k % (rows // step) * step if isinstance(k, int) else lax.rem(k, rows // step) * step
                stores += fn(p, r, step)
            for ref, at, value in stores:
                ref[at] = value
            return 0
        if turns == per:
            body(0, 0)
        else:
            lax.fori_loop(0, turns // per, body, 0)

    def strip(base, step):
        return pl.ds(base if isinstance(base, int) else pl.multiple_of(base, 16), step)

    def reduce_chain(group, base, rows, n, at, plus, minus, off, bufs):
        out_p1, out_m1, out_p2, out_m2, in_p1, in_m1, in_p2, in_m2 = bufs
        far = n // 2
        first, count, column, columns = group
        some, window, every = pl.ds(first, count), pl.ds(off, rows), pl.ds(column, columns)
        left, right = pl.ds(column, columns // 2), pl.ds(column + columns // 2, columns // 2)
        short = pl.ds(column // 2, columns // 2)

        def pack(s, source, cols, out1, out2, in1, in2):
            rest = right if cols is left else left
            def fn(p, r, step):
                there = strip(source + r, step)
                here = strip(off + r, step)
                if s == 1:
                    return [(out1, (p, here, short), encode(part[p, there, cols]))]
                if s > 2:
                    value = encode(part[p, there, every] + decode(in2[s - 3, p, here, every]))
                    return [(out2, (s - 2, p, here, every), value)]
                value = encode(part[p, there, cols] + decode(in1[p, here, short]))
                return [
                    (out2, (0, p, here, cols), value),
                    (out2, (0, p, here, rest), encode(part[p, there, rest])),
                ]
            return fn

        for s in range(1, far + 1):
            distance = far + 1 - s
            go_p = pack(s, base + lax.rem(at + distance, n) * rows, left, out_p1, out_p2, in_p1, in_p2)
            go_m = pack(s, base + lax.rem(at + n - distance, n) * rows, right, out_m1, out_m2, in_m1, in_m2)
            sweep(group, rows, lambda p, r, step: go_p(p, r, step) + go_m(p, r, step))
            def view(ref1, ref2):
                return ref1.at[some, window, short] if s == 1 else ref2.at[s - 2, some, window, every]
            go = [
                send(view(out_p1, out_p2), view(in_p1, in_p2), plus),
                send(view(out_m1, out_m2), view(in_m1, in_m2), minus),
            ]
            yield
            arrive(go)

        def finish(p, r, step):
            there = strip(base + at * rows + r, step)
            here = strip(off + r, step)
            value = part[p, there, every] + decode(in_p2[far - 2, p, here, every])
            return [(part, (p, there, every), value + decode(in_m2[far - 2, p, here, every]))]
        sweep(group, rows, finish)

    def gather_chain(group, base, rows, n, at, plus, minus):
        far = n // 2
        first, count, column, columns = group
        some, every = pl.ds(first, count), pl.ds(column, columns)
        left, right = pl.ds(column, columns // 2), pl.ds(column + columns // 2, columns // 2)
        for s in range(1, far + 1):
            cols_p, cols_m = (left, right) if s == far else (every, every)
            from_p = base + lax.rem(at + n - (s - 1), n) * rows
            from_m = base + lax.rem(at + (s - 1), n) * rows
            ref_p = slope.at[some, strip(from_p, rows), cols_p]
            ref_m = slope.at[some, strip(from_m, rows), cols_m]
            go = [send(ref_p, ref_p, plus), send(ref_m, ref_m, minus)]
            yield
            arrive(go)

    plus_x, minus_x = device(dx=1), device(dx=nx - 1)
    plus_z, minus_z = device(dz=1), device(dz=nz - 1)
    top = width // 2
    rows_x, rows_z, rows_o = top // nx, top // nz, top // (nx * nz)
    base_x = x * rows_x
    base_z = top + z * rows_z
    bufs_x = (sx_p1, sx_m1, sx_p2, sx_m2, rx_p1, rx_m1, rx_p2, rx_m2)
    bufs_z = (sz_p1, sz_m1, sz_p2, sz_m2, rz_p1, rz_m1, rz_p2, rz_m2)

    def slopes(group, base):
        first, count, column, columns = group
        rows, cols = strip(base, rows_o), pl.ds(column, columns)
        row_ids = lax.broadcasted_iota(jnp.int32, (rows_o, columns), 0) + base
        col_ids = lax.broadcasted_iota(jnp.int32, (rows_o, columns), 1) + (c * half + column)
        for p in range(first, first + count):
            value = 2.0 * off_weight * (part[p, rows, cols] / total)
            if p == 0:
                value = jnp.where(row_ids == col_ids, 0.0, value)
            slope[p, rows, cols] = value.astype(bf16)

    def one_way(group):
        yield from reduce_chain(group, 0, rows_x, nx, x, plus_x, minus_x, 0, bufs_x)
        yield from reduce_chain(group, base_x, rows_o, nz, z, plus_z, minus_z, rows_z, bufs_z)
        slopes(group, base_x + z * rows_o)
        yield from gather_chain(group, base_x, rows_o, nz, z, plus_z, minus_z)
        yield from gather_chain(group, 0, rows_x, nx, x, plus_x, minus_x)

    def other_way(group):
        yield from reduce_chain(group, top, rows_z, nz, z, plus_z, minus_z, 0, bufs_z)
        yield from reduce_chain(group, base_z, rows_o, nx, x, plus_x, minus_x, rows_x, bufs_x)
        slopes(group, base_z + x * rows_o)
        yield from gather_chain(group, base_z, rows_o, nx, x, plus_x, minus_x)
        yield from gather_chain(group, top, rows_z, nz, z, plus_z, minus_z)

    def step_all(live):
        for chain in list(live):
            if next(chain, live) is live:
                live.remove(chain)

    def to_b(group):
        first, count, column, columns = group
        for p in range(first, first + count):
            def body(i, _, p=p):
                cols = pl.ds(pl.multiple_of(column + i * 256, 256), 256)
                part_b[p, :, cols] = jnp.dot(na[...], slope[p, :, cols], preferred_element_type=f32)
                return 0
            if columns == 256:
                cols = pl.ds(column, 256)
                part_b[p, :, cols] = jnp.dot(na[...], slope[p, :, cols], preferred_element_type=f32)
            else:
                lax.fori_loop(0, columns // 256, body, 0)

    begun = []

    def to_a(group):
        first, count, column, columns = group
        cols = pl.ds(column, columns)
        fresh = not begun
        begun.append(group)
        def body(i, _):
            rows = pl.ds(pl.multiple_of(i * 256, 256), 256)
            acc = None if fresh else back_a[:, rows]
            for p in range(first, first + count):
                term = lax.dot_general(
                    nb[p, :, cols], slope[p, rows, cols], (((1,), (1,)), ((), ())),
                    preferred_element_type=f32)
                acc = term if acc is None else acc + term
            back_a[:, rows] = acc
            return 0
        lax.fori_loop(0, width // 256, body, 0)

    def squares(group):
        first, count, column, columns = group
        cols = pl.ds(column, columns)
        for p in range(first, first + count):
            def body(i, acc, p=p):
                rows = pl.ds(pl.multiple_of(i * 32, 32), 32)
                s = slope[p, rows, cols].astype(f32)
                s = s * s
                row_acc[rows, :] += sum(s[:, k * 128 : (k + 1) * 128] for k in range(columns // 128))
                return acc + jnp.sum(s, axis=0, keepdims=True)
            square[p, :, cols] = lax.fori_loop(0, width // 32, body, jnp.zeros((1, columns), f32))

    def whole(group):
        live = [one_way(group), other_way(group)]
        while live:
            step_all(live)
            if live:
                yield

    far_y, near_y = [], []

    def group_own():
        yield from whole(GROUP_OWN)
        squares(GROUP_OWN)
        to_b(GROUP_OWN)
        to_a(GROUP_OWN)

    def group_far():
        yield from whole(GROUP_FAR)
        to_b(GROUP_FAR)
        def body(i, _):
            here = pl.ds(pl.multiple_of(i * 32, 32), 32)
            there = pl.ds(pl.multiple_of(i * 32 + frames, 32), 32)
            sy_p1[here, :] = encode(part_b[3, here, :])
            sy_m1[here, :] = encode(part_b[3, there, :])
            return 0
        lax.fori_loop(0, frames // 32, body, 0)
        far_y.extend([send(sy_p1, ry_p1, up), send(sy_m1, ry_m1, down)])
        to_a(GROUP_FAR)
        squares(GROUP_FAR)

    def group_near(group):
        yield from whole(group)
        to_b(group)
        if not near_y:
            arrive(far_y)
        cols = pl.ds(group[2], group[3])
        def body(i, _):
            here = pl.ds(pl.multiple_of(i * 32, 32), 32)
            there = pl.ds(pl.multiple_of(i * 32 + frames, 32), 32)
            plus_near = encode(part_b[1, here, cols] + decode(ry_p1[here, cols]))
            plus_rest = encode(part_b[1, there, cols])
            minus_rest = encode(part_b[2, here, cols])
            minus_near = encode(part_b[2, there, cols] + decode(ry_m1[here, cols]))
            sy_p2[here, cols] = plus_near
            sy_p2[there, cols] = plus_rest
            sy_m2[here, cols] = minus_rest
            sy_m2[there, cols] = minus_near
            return 0
        lax.fori_loop(0, frames // 32, body, 0)
        near_y.append([
            send(sy_p2.at[:, cols], ry_p2.at[:, cols], up),
            send(sy_m2.at[:, cols], ry_m2.at[:, cols], down),
        ])
        to_a(group)
        squares(group)

    GROUP_OWN, GROUP_FAR = (0, 1, 0, half), (3, 1, 0, half)
    NEAR = [(1, 2, 0, half // 2), (1, 2, half // 2, half // 2)]

    row_acc[...] = jnp.zeros_like(row_acc)
    diag_chain = diagonal()
    swap_a.wait_recv()
    for i in range(width // 128):
        cols = pl.ds(i * 128, 128)
        nat[cols, :] = jnp.transpose(na[:both, cols].astype(f32)).astype(bf16)
    correlate(0)
    live = [group_own()]
    step_all(live)
    next(diag_chain)
    arrive(first)
    second = [
        send(nb.at[2, own], nb.at[3, own], up),
        send(nb.at[1, other], nb.at[3, other], down),
    ]
    third = [
        send(nb.at[0, other], nb.at[2, other], up),
        send(nb.at[0, own], nb.at[1, own], down),
    ]
    step_all(live)
    next(diag_chain)
    step_all(live)
    next(diag_chain)
    step_all(live)
    arrive(second)
    correlate(3)
    live.append(group_far())
    step_all(live)
    next(diag_chain)
    step_all(live)
    arrive(third)
    correlate(1)
    correlate(2)
    live += [group_near(group) for group in NEAR]
    step_all(live)
    next(diag_chain, None)
    while live:
        step_all(live)

    swap_back = send(back_a.at[other, :], recv_a, partner)

    scale = 1.0 / (2.0 * off_weight)
    corr_half = diag_f[c, 1, 0:1]
    loss_off = jnp.sum(sum(square[p] for p in range(slots)), axis=1, keepdims=True)
    loss_diag = jnp.sum((1.0 - corr_half) ** 2, axis=1, keepdims=True)
    loss_row = jnp.broadcast_to(loss_off * (off_weight * scale * scale) + loss_diag, (1, half))
    for p in range(slots):
        block = extra_y.at[ny + p] if p else extra_y.at[m]
        block[0:1, :] = part_b[p, both : both + 1, :]
        block[1:2, :] = square[p] * scale
        block[2:3, :] = loss_row
        block[3:4, :] = jnp.zeros((1, half), f32)
    share_y = [
        send(extra_y.at[ny + SLOT[k]], extra_y.at[m], peers_y[k - 1]) for k in range(1, ny)
    ]
    extra_a[c, 0:1, :] = back_a[both : both + 1, :]
    extra_a[c, 1:2, :] = jnp.sum(jnp.transpose(row_acc[...]), axis=0, keepdims=True) * scale
    share_a = send(extra_a.at[c], extra_a.at[c], partner)

    diag = jnp.concatenate([diag_f[0], diag_f[1]], axis=2)
    mean_a16, mean_own_b16 = diag[0, 0:1], diag[0, 1:2]
    corr_ii = diag[1, 0:1]
    cross_a, cross_b = diag[2, 0:1], diag[2, 1:2]
    slope_ii = (-2.0 * (1.0 - corr_ii)).astype(bf16).astype(f32)

    share_a.wait_recv()
    last_a = extra_a[0] + extra_a[1]
    mean_a = last_a[0:1] + mean_own_b16 * slope_ii
    inner_a = last_a[1:2] + cross_a * slope_ii
    swap_back.wait_recv()

    def finish_a(i, _):
        rows = pl.ds(pl.multiple_of(i * 32, 32), 32)
        wide = (a_ref[rows, :].astype(f32) - center_a) * inv_a
        back = back_a[rows, :] + recv_a[rows, :] + slope_ii * nb16[rows, :].astype(f32)
        ga_ref[rows, :] = (inv_a * (back - mean_a - wide * inner_a)).astype(bf16)
        return 0

    lax.fori_loop(0, frames // 32, finish_a, 0)

    arrive(share_y)
    extra_c[c] = sum(extra_y[i] for i in range(ny))
    share_c = send(extra_c.at[c], extra_c.at[c], partner)

    def add_last(base, cols):
        def body(i, _):
            rows = pl.ds(pl.multiple_of(base + i * 64, 64), 64)
            sum_b[rows, cols] = (
                part_b[0, rows, cols] + decode(ry_p2[rows, cols]) + decode(ry_m2[rows, cols])
            )
            return 0
        lax.fori_loop(0, frames // 64, body, 0)

    swap_sum = []
    for group, copies in zip(NEAR, near_y):
        arrive(copies)
        cols = pl.ds(group[2], group[3])
        there = pl.ds(pl.multiple_of(c * half + group[2], 128), group[3])
        add_last(frames, cols)
        swap_sum.append(send(sum_b.at[other, cols], full_b.at[:, there], partner))
        add_last(0, cols)
        full_b[:, there] = sum_b[own, cols]

    share_c.wait_recv()
    mean_b = jnp.concatenate([extra_c[0, 0:1], extra_c[1, 0:1]], axis=1) + mean_a16 * slope_ii
    inner_b = jnp.concatenate([extra_c[0, 1:2], extra_c[1, 1:2]], axis=1) + cross_b * slope_ii
    loss_ref[...] = jnp.broadcast_to(extra_c[0, 2:3, :128] + extra_c[1, 2:3, :128], (8, 128))
    arrive(swap_sum)

    def finish_b(i, _):
        rows = pl.ds(pl.multiple_of(i * 32, 32), 32)
        wide = (b_ref[rows, :].astype(f32) - center_b) * inv_b
        back = full_b[rows, :] + slope_ii * na[rows, :].astype(f32)
        gb_ref[rows, :] = (inv_b * (back - mean_b - wide * inner_b)).astype(bf16)
        return 0

    lax.fori_loop(0, frames // 32, finish_b, 0)
    for copy in started:
        copy.wait_send()


def solution(mesh):
    ny = mesh.shape["mp"]
    members = mesh.shape["dp"]
    nx = ny
    nz = members // (2 * nx)

    def per_device(view_a, view_b):
        frames, width = view_a.shape
        both, half = 2 * frames, width // 2
        quarter = half // 2
        top = width // 2
        rows_x, rows_z, rows_o = top // nx, top // nz, top // (nx * nz)
        vmem = pltpu.VMEM
        rings = []
        scratch = [
            vmem((frames, width), bf16),
            vmem((both + 16, width), bf16),
            vmem((width, both), bf16),
            vmem((ny, both + 16, half), bf16),
            vmem((ny, width, half), f32),
            vmem((ny, width, half), bf16),
            vmem((both + 16, width), f32),
            vmem((ny, both + 16, half), f32),
            vmem((both, half), f32),
            vmem((frames, width), f32),
            vmem((2, 2, 2, width), f32),
            vmem((nx, 2, 2, width), f32),
            vmem((nz, 2, 2, width), f32),
            vmem((2, 3, 2, width), f32),
            vmem((nx, 3, 2, half), f32),
            vmem((nz, 3, 2, half), f32),
            vmem((2, 3, 2, half), f32),
            vmem((ny, 1, half), f32),
            vmem((ny, 1, half), f32),
            vmem((2 * ny, 4, half), f32),
            vmem((2, 4, half), f32),
            vmem((2, 2, width), f32),
            vmem((width, 128), f32),
        ]
        for rows, n in ((rows_x + rows_o, nx), (rows_z + rows_o, nz)):
            ring = [vmem((ny, rows, quarter), bf16)] * 2 + [vmem((n // 2 - 1, ny, rows, half), bf16)] * 2
            rings.append(ring)
        ring_y = [vmem((frames, half), bf16)] * 2 + [vmem((both, half), bf16)] * 2
        scratch += rings[0] + rings[1] + rings[0] + rings[1] + ring_y + ring_y + [
            vmem((frames, width), f32),
            pltpu.SemaphoreType.DMA((256,)),
            pltpu.SemaphoreType.DMA((256,)),
        ]
        grad_a, grad_b, loss = pl.pallas_call(
            functools.partial(kernel, nx, nz, ny, float(frames * members)),
            out_shape=(
                jax.ShapeDtypeStruct((frames, width), bf16),
                jax.ShapeDtypeStruct((frames, width), bf16),
                jax.ShapeDtypeStruct((8, 128), f32),
            ),
            in_specs=[pl.BlockSpec(memory_space=vmem)] * 2,
            out_specs=[pl.BlockSpec(memory_space=vmem)] * 3,
            scratch_shapes=scratch,
            compiler_params=pltpu.CompilerParams(
                collective_id=0, has_side_effects=True, vmem_limit_bytes=56 * 1024 * 1024
            ),
            cost_estimate=pl.CostEstimate(
                flops=3 * 2 * both * width * half * ny, bytes_accessed=4 * frames * width * 2,
                transcendentals=0),
        )(view_a, view_b)
        return grad_a, grad_b, loss[0, 0]

    placed = P("dp", "mp")
    return jax.shard_map(
        per_device,
        mesh=mesh,
        in_specs=(placed, placed),
        out_specs=(placed, placed, P()),
        check_vma=False,
    )
```

time: 174 us -> 143 us (0.82)
  Pallas kernels: 168 us -> 138 us
    pallas_call x1, Pallas kernels: 168 us -> 138 us  [per_device(): pl.pallas_call(functools.partial(kernel, nx, nz, ny, float(frames * membe...]
where the time goes in v2:
time: 143 us
  Pallas kernels  138 us (97%)
  local copies, waits for them, and re-layouts  4.06 us (3%)
    pallas_call x1, Pallas kernels, per_device(): pl.pallas_call(functools.partial(kernel, nx, nz, ny, float(frames * membe...  138 us
    unnamed x4, local copies, waits for them, and re-layouts  2.87 us

profile of v2, /device:TPU:1, one launch (start us, length us, event | category | flops | bytes accessed | tf_op | source)
XLA Modules:
  0.0 142.9 jit_solution(18104849356840519275)
XLA Ops:
  0.6 138.2 %shard_map.49 = (bf16[320,1024]{1,0:T(8,128)(2,1)}, bf16[320,1024]{1,0:T(8,128)(2,1)}, f32[8,128]{1,0:T(8,128)}) custom-call(bf16[320,1024]{1,0:T(8,128)(2,1)} %a_ref.1, bf16[320,1024]{1,0:T(8,128)(2,1)} %b_ref.1), custom_call_target="tpu_custom_call" | custom-call | flops 8053063680 | bytes 2621440 | tf_op jit(solution)/shard_map/pallas_call | solution.py:586
  138.8 1.2 slice.3
  140.0 0.0 copy-start
  140.0 2.0 %copy.7 = bf16[320,1024]{1,0:T(8,128)(2,1)} copy(bf16[320,1024]{1,0:T(8,128)(2,1)} %get-tuple-element.12) | data formatting | bytes 1310720
  142.0 0.0 copy-done
  142.0 0.8 copy.8
Async XLA Ops:
  140.0 2.0 %copy-start = (bf16[320,1024]{1,0:T(8,128)(2,1)S(1)}, bf16[320,1024]{1,0:T(8,128)(2,1)}, u32[]{:S(2)}) copy-start(bf16[320,1024]{1,0:T(8,128)(2,1)} %get-tuple-element.13) | copy-start | bytes 1966084

commit v3 on v2

--- a/solution.py
+++ b/solution.py
@@ -71,10 +71,22 @@
     for peer in everyone:
         pl.semaphore_signal(barrier, inc=1, device_id=peer, device_id_type=MESH)
 
-    started = []
-
-    def send(src, dst, peer):
+    started, due, clock, free = [], {}, [0.0], {}
+
+    def work(t):
+        clock[0] += t
+
+    def send(src, dst, peer, link=None):
         at = len(started)
+        work(0.2)
+        size = src.dtype.itemsize
+        for d in src.shape:
+            size *= d
+        rate = 45e3 if link else 500e3
+        begin = max(clock[0], free.get(link, 0.0)) if link else clock[0]
+        end = begin + size / rate
+        if link:
+            free[link] = end
         copy = pltpu.make_async_remote_copy(
             src_ref=src,
             dst_ref=dst,
@@ -85,10 +97,12 @@
         )
         copy.start()
         started.append(copy)
+        due[id(copy)] = end + 1.5
         return copy
 
     def arrive(copies):
         for copy in copies:
+            clock[0] = max(clock[0], due[id(copy)])
             copy.wait_recv()
 
     def spread_to(buf, mine, peers):
@@ -141,11 +155,13 @@
     swap_b = send(nb16.at[:, other_half], nb.at[0, other], partner)
     nb[0, own, :] = nb16[:, own_half]
     up, down = device(dy=1), device(dy=ny - 1)
-    first = [send(nb.at[0, own], nb.at[2, own], up)]
+    first = [send(nb.at[0, own], nb.at[2, own], up, "y+")]
     standardize(a_ref, na, center_a, inv_a)
     swap_a = send(na.at[own], na.at[other], partner)
-    swap_b.wait_recv()
-    first.append(send(nb.at[0, other], nb.at[1, other], down))
+    arrive([swap_b])
+    first.append(send(nb.at[0, other], nb.at[1, other], down, "y-"))
+
+    diag_done = []
 
     def diagonal():
         def body(i, acc):
@@ -158,31 +174,30 @@
         sums = lax.fori_loop(0, frames // 32, body, (jnp.zeros((1, width), f32),) * 5)
         for at, value in enumerate(sums[:3] + (jnp.zeros((1, width), f32),) + sums[3:]):
             diag_c[c, at // 2, at % 2 : at % 2 + 1, :] = value
+        work(1.5)
         copies = spread_to(diag_c, c, [partner])
-        yield
-        arrive(copies)
+        yield copies
         diag_x[x] = jnp.where(
             c == 0, diag_c[0, :, :, :half] + diag_c[1, :, :, :half],
             diag_c[0, :, :, half:] + diag_c[1, :, :, half:])
         copies = spread_to(diag_x, x, peers_x)
-        yield
-        arrive(copies)
+        yield copies
         diag_z[z] = sum(diag_x[i] for i in range(nx))
         copies = spread_to(diag_z, z, peers_z)
-        yield
-        arrive(copies)
+        yield copies
         diag_f[c] = sum(diag_z[i] for i in range(nz)) / total
         mean_b16[0] = diag_f[c, 0, 1:2]
         copies = spread_to(diag_f, c, [partner])
         copies += [send(mean_b16.at[0], mean_b16.at[SLOT[ny - k]], peers_y[k - 1]) for k in range(1, ny)]
-        yield
-        arrive(copies)
+        yield copies
         mean_a = jnp.concatenate([diag_f[0, 0, 0:1], diag_f[1, 0, 0:1]], axis=1)
         na[pl.ds(both, 16), :] = jnp.broadcast_to(mean_a, (16, width)).astype(bf16)
         for p in range(slots):
             nb[p, pl.ds(both, 16), :] = jnp.broadcast_to(mean_b16[p], (16, half)).astype(bf16)
+        diag_done.append(True)
 
     def correlate(p):
+        work(1.5)
         def body(i, _):
             rows = pl.ds(pl.multiple_of(i * 256, 256), 256)
             part[p, rows, :] = jnp.dot(nat[rows, :], nb[p, :both, :], preferred_element_type=f32)
@@ -191,6 +206,7 @@
 
     def sweep(group, rows, fn):
         first, count, _, columns = group
+        work(0.004 * rows * count * columns / 1024)
         step = min(rows, 32)
         turns = count * (rows // step)
         per = min(turns, max(1, 16384 // (step * columns)))
@@ -212,7 +228,7 @@
     def strip(base, step):
         return pl.ds(base if isinstance(base, int) else pl.multiple_of(base, 16), step)
 
-    def reduce_chain(group, base, rows, n, at, plus, minus, off, bufs):
+    def reduce_chain(group, base, rows, n, at, plus, minus, axis, off, bufs):
         out_p1, out_m1, out_p2, out_m2, in_p1, in_m1, in_p2, in_m2 = bufs
         far = n // 2
         first, count, column, columns = group
@@ -245,11 +261,10 @@
             def view(ref1, ref2):
                 return ref1.at[some, window, short] if s == 1 else ref2.at[s - 2, some, window, every]
             go = [
-                send(view(out_p1, out_p2), view(in_p1, in_p2), plus),
-                send(view(out_m1, out_m2), view(in_m1, in_m2), minus),
+                send(view(out_p1, out_p2), view(in_p1, in_p2), plus, axis + "+"),
+                send(view(out_m1, out_m2), view(in_m1, in_m2), minus, axis + "-"),
             ]
-            yield
-            arrive(go)
+            yield go
 
         def finish(p, r, step):
             there = strip(base + at * rows + r, step)
@@ -258,7 +273,7 @@
             return [(part, (p, there, every), value + decode(in_m2[far - 2, p, here, every]))]
         sweep(group, rows, finish)
 
-    def gather_chain(group, base, rows, n, at, plus, minus):
+    def gather_chain(group, base, rows, n, at, plus, minus, axis):
         far = n // 2
         first, count, column, columns = group
         some, every = pl.ds(first, count), pl.ds(column, columns)
@@ -269,16 +284,13 @@
             from_m = base + lax.rem(at + (s - 1), n) * rows
             ref_p = slope.at[some, strip(from_p, rows), cols_p]
             ref_m = slope.at[some, strip(from_m, rows), cols_m]
-            go = [send(ref_p, ref_p, plus), send(ref_m, ref_m, minus)]
-            yield
-            arrive(go)
+            yield [send(ref_p, ref_p, plus, axis + "+"), send(ref_m, ref_m, minus, axis + "-")]
 
     plus_x, minus_x = device(dx=1), device(dx=nx - 1)
     plus_z, minus_z = device(dz=1), device(dz=nz - 1)
-    top = width // 2
-    rows_x, rows_z, rows_o = top // nx, top // nz, top // (nx * nz)
+    rows_x, rows_z, rows_o = width // nx, width // nz, width // (nx * nz)
     base_x = x * rows_x
-    base_z = top + z * rows_z
+    base_z = z * rows_z
     bufs_x = (sx_p1, sx_m1, sx_p2, sx_m2, rx_p1, rx_m1, rx_p2, rx_m2)
     bufs_z = (sz_p1, sz_m1, sz_p2, sz_m2, rz_p1, rz_m1, rz_p2, rz_m2)
 
@@ -294,26 +306,55 @@
             slope[p, rows, cols] = value.astype(bf16)
 
     def one_way(group):
-        yield from reduce_chain(group, 0, rows_x, nx, x, plus_x, minus_x, 0, bufs_x)
-        yield from reduce_chain(group, base_x, rows_o, nz, z, plus_z, minus_z, rows_z, bufs_z)
+        yield from reduce_chain(group, 0, rows_x, nx, x, plus_x, minus_x, "x", 0, bufs_x)
+        yield from reduce_chain(group, base_x, rows_o, nz, z, plus_z, minus_z, "z", rows_z, bufs_z)
         slopes(group, base_x + z * rows_o)
-        yield from gather_chain(group, base_x, rows_o, nz, z, plus_z, minus_z)
-        yield from gather_chain(group, 0, rows_x, nx, x, plus_x, minus_x)
+        yield from gather_chain(group, base_x, rows_o, nz, z, plus_z, minus_z, "z")
+        yield from gather_chain(group, 0, rows_x, nx, x, plus_x, minus_x, "x")
 
     def other_way(group):
-        yield from reduce_chain(group, top, rows_z, nz, z, plus_z, minus_z, 0, bufs_z)
-        yield from reduce_chain(group, base_z, rows_o, nx, x, plus_x, minus_x, rows_x, bufs_x)
+        yield from reduce_chain(group, 0, rows_z, nz, z, plus_z, minus_z, "z", 0, bufs_z)
+        yield from reduce_chain(group, base_z, rows_o, nx, x, plus_x, minus_x, "x", rows_x, bufs_x)
         slopes(group, base_z + x * rows_o)
-        yield from gather_chain(group, base_z, rows_o, nx, x, plus_x, minus_x)
-        yield from gather_chain(group, top, rows_z, nz, z, plus_z, minus_z)
-
-    def step_all(live):
-        for chain in list(live):
-            if next(chain, live) is live:
-                live.remove(chain)
+        yield from gather_chain(group, base_z, rows_o, nx, x, plus_x, minus_x, "x")
+        yield from gather_chain(group, 0, rows_z, nz, z, plus_z, minus_z, "z")
+
+    live = []
+
+    def spawn(rank, task):
+        live.append([rank, len(started), task, []])
+
+    def run():
+        while live:
+            best = None
+            for entry in live:
+                rank, _, _, wait = entry
+                if callable(wait):
+                    if not wait():
+                        continue
+                    ready = clock[0]
+                else:
+                    ready = max([clock[0]] + [due[id(copy)] for copy in wait])
+                key = (max(ready, clock[0] + 0.2), rank)
+                if best is None or key < best[0]:
+                    best = (key, entry)
+            entry = best[1]
+            if not callable(entry[3]):
+                arrive(entry[3])
+            entry[3] = next(entry[2], None)
+            if entry[3] is None:
+                live.remove(entry)
+
+    def group(rank, way, what, post):
+        def chain():
+            yield from way(what)
+            yield lambda: diag_done
+            yield from post
+        spawn(rank, chain())
 
     def to_b(group):
         first, count, column, columns = group
+        work(1.5 * count * columns / half)
         for p in range(first, first + count):
             def body(i, _, p=p):
                 cols = pl.ds(pl.multiple_of(column + i * 256, 256), 256)
@@ -331,6 +372,7 @@
         first, count, column, columns = group
         cols = pl.ds(column, columns)
         fresh = not begun
+        work(0.5 + 1.5 * count * columns / half)
         begun.append(group)
         def body(i, _):
             rows = pl.ds(pl.multiple_of(i * 256, 256), 256)
@@ -346,6 +388,7 @@
 
     def squares(group):
         first, count, column, columns = group
+        work(0.6 * count * columns / half)
         cols = pl.ds(column, columns)
         for p in range(first, first + count):
             def body(i, acc, p=p):
@@ -356,102 +399,87 @@
                 return acc + jnp.sum(s, axis=0, keepdims=True)
             square[p, :, cols] = lax.fori_loop(0, width // 32, body, jnp.zeros((1, columns), f32))
 
-    def whole(group):
-        live = [one_way(group), other_way(group)]
-        while live:
-            step_all(live)
-            if live:
-                yield
-
-    far_y, near_y = [], []
-
-    def group_own():
-        yield from whole(GROUP_OWN)
-        squares(GROUP_OWN)
-        to_b(GROUP_OWN)
-        to_a(GROUP_OWN)
-
-    def group_far():
-        yield from whole(GROUP_FAR)
-        to_b(GROUP_FAR)
+    far_ready, near_y = [], []
+
+    def wait_far(copies):
+        yield copies
+        far_ready.append(True)
+
+    def post_own():
+        to_b(OWN)
+        to_a(OWN)
+        squares(OWN)
+        yield []
+
+    def post_far():
+        to_b(FAR)
+        work(1.0)
         def body(i, _):
             here = pl.ds(pl.multiple_of(i * 32, 32), 32)
             there = pl.ds(pl.multiple_of(i * 32 + frames, 32), 32)
-            sy_p1[here, :] = encode(part_b[3, here, :])
-            sy_m1[here, :] = encode(part_b[3, there, :])
+            plus, minus = encode(part_b[3, here, :]), encode(part_b[3, there, :])
+            sy_p1[here, :] = plus
+            sy_m1[here, :] = minus
             return 0
         lax.fori_loop(0, frames // 32, body, 0)
-        far_y.extend([send(sy_p1, ry_p1, up), send(sy_m1, ry_m1, down)])
-        to_a(GROUP_FAR)
-        squares(GROUP_FAR)
-
-    def group_near(group):
-        yield from whole(group)
-        to_b(group)
-        if not near_y:
-            arrive(far_y)
-        cols = pl.ds(group[2], group[3])
+        spawn(0, wait_far([send(sy_p1, ry_p1, up, "y+"), send(sy_m1, ry_m1, down, "y-")]))
+        yield []
+        to_a(FAR)
+        squares(FAR)
+
+    def post_near(what, out, got, into, peer, link, near, rest):
+        to_b(what)
+        yield lambda: far_ready
+        work(1.0)
+        p = what[0]
         def body(i, _):
             here = pl.ds(pl.multiple_of(i * 32, 32), 32)
-            there = pl.ds(pl.multiple_of(i * 32 + frames, 32), 32)
-            plus_near = encode(part_b[1, here, cols] + decode(ry_p1[here, cols]))
-            plus_rest = encode(part_b[1, there, cols])
-            minus_rest = encode(part_b[2, here, cols])
-            minus_near = encode(part_b[2, there, cols] + decode(ry_m1[here, cols]))
-            sy_p2[here, cols] = plus_near
-            sy_p2[there, cols] = plus_rest
-            sy_m2[here, cols] = minus_rest
-            sy_m2[there, cols] = minus_near
+            rows_n = pl.ds(pl.multiple_of(i * 32 + near, 32), 32)
+            rows_r = pl.ds(pl.multiple_of(i * 32 + rest, 32), 32)
+            first_half = encode(part_b[p, rows_n, :] + decode(got[here, :]))
+            other_part = encode(part_b[p, rows_r, :])
+            out[rows_n, :] = first_half
+            out[rows_r, :] = other_part
             return 0
         lax.fori_loop(0, frames // 32, body, 0)
-        near_y.append([
-            send(sy_p2.at[:, cols], ry_p2.at[:, cols], up),
-            send(sy_m2.at[:, cols], ry_m2.at[:, cols], down),
-        ])
-        to_a(group)
-        squares(group)
-
-    GROUP_OWN, GROUP_FAR = (0, 1, 0, half), (3, 1, 0, half)
-    NEAR = [(1, 2, 0, half // 2), (1, 2, half // 2, half // 2)]
+        near_y.append(send(out, into, peer, link))
+        yield []
+        to_a(what)
+        squares(what)
+
+    OWN, UP, DOWN, FAR = ((p, 1, 0, half) for p in range(slots))
+
+    def blocks():
+        yield first
+        second = [
+            send(nb.at[2, own], nb.at[3, own], up, "y+"),
+            send(nb.at[1, other], nb.at[3, other], down, "y-"),
+        ]
+        third = [
+            send(nb.at[0, other], nb.at[2, other], up, "y+"),
+            send(nb.at[0, own], nb.at[1, own], down, "y-"),
+        ]
+        yield second
+        correlate(3)
+        group(2, one_way, FAR, post_far())
+        yield third
+        correlate(1)
+        group(1, other_way, UP, post_near(UP, sy_p2, ry_p1, ry_p2, up, "y+", 0, frames))
+        yield []
+        correlate(2)
+        group(1, one_way, DOWN, post_near(DOWN, sy_m2, ry_m1, ry_m2, down, "y-", frames, 0))
 
     row_acc[...] = jnp.zeros_like(row_acc)
-    diag_chain = diagonal()
-    swap_a.wait_recv()
+    arrive([swap_a])
     for i in range(width // 128):
         cols = pl.ds(i * 128, 128)
         nat[cols, :] = jnp.transpose(na[:both, cols].astype(f32)).astype(bf16)
+    work(2.0)
     correlate(0)
-    live = [group_own()]
-    step_all(live)
-    next(diag_chain)
-    arrive(first)
-    second = [
-        send(nb.at[2, own], nb.at[3, own], up),
-        send(nb.at[1, other], nb.at[3, other], down),
-    ]
-    third = [
-        send(nb.at[0, other], nb.at[2, other], up),
-        send(nb.at[0, own], nb.at[1, own], down),
-    ]
-    step_all(live)
-    next(diag_chain)
-    step_all(live)
-    next(diag_chain)
-    step_all(live)
-    arrive(second)
-    correlate(3)
-    live.append(group_far())
-    step_all(live)
-    next(diag_chain)
-    step_all(live)
-    arrive(third)
-    correlate(1)
-    correlate(2)
-    live += [group_near(group) for group in NEAR]
-    step_all(live)
-    next(diag_chain, None)
-    while live:
-        step_all(live)
+    spawn(0, blocks())
+    group(3, one_way, OWN, post_own())
+    spawn(2, diagonal())
+    run()
 
     swap_back = send(back_a.at[other, :], recv_a, partner)
 
@@ -479,11 +507,11 @@
     cross_a, cross_b = diag[2, 0:1], diag[2, 1:2]
     slope_ii = (-2.0 * (1.0 - corr_ii)).astype(bf16).astype(f32)
 
-    share_a.wait_recv()
+    arrive([share_a])
     last_a = extra_a[0] + extra_a[1]
     mean_a = last_a[0:1] + mean_own_b16 * slope_ii
     inner_a = last_a[1:2] + cross_a * slope_ii
-    swap_back.wait_recv()
+    arrive([swap_back])
 
     def finish_a(i, _):
         rows = pl.ds(pl.multiple_of(i * 32, 32), 32)
@@ -498,26 +526,20 @@
     extra_c[c] = sum(extra_y[i] for i in range(ny))
     share_c = send(extra_c.at[c], extra_c.at[c], partner)
 
-    def add_last(base, cols):
+    def add_last(base):
         def body(i, _):
-            rows = pl.ds(pl.multiple_of(base + i * 64, 64), 64)
-            sum_b[rows, cols] = (
-                part_b[0, rows, cols] + decode(ry_p2[rows, cols]) + decode(ry_m2[rows, cols])
-            )
+            rows = pl.ds(pl.multiple_of(base + i * 32, 32), 32)
+            sum_b[rows, :] = part_b[0, rows, :] + decode(ry_p2[rows, :]) + decode(ry_m2[rows, :])
             return 0
-        lax.fori_loop(0, frames // 64, body, 0)
-
-    swap_sum = []
-    for group, copies in zip(NEAR, near_y):
-        arrive(copies)
-        cols = pl.ds(group[2], group[3])
-        there = pl.ds(pl.multiple_of(c * half + group[2], 128), group[3])
-        add_last(frames, cols)
-        swap_sum.append(send(sum_b.at[other, cols], full_b.at[:, there], partner))
-        add_last(0, cols)
-        full_b[:, there] = sum_b[own, cols]
-
-    share_c.wait_recv()
+        lax.fori_loop(0, frames // 32, body, 0)
+
+    arrive(near_y)
+    add_last(frames)
+    swap_sum = [send(sum_b.at[other, :], full_b.at[:, own_half], partner)]
+    add_last(0)
+    full_b[:, own_half] = sum_b[own, :]
+
+    arrive([share_c])
     mean_b = jnp.concatenate([extra_c[0, 0:1], extra_c[1, 0:1]], axis=1) + mean_a16 * slope_ii
     inner_b = jnp.concatenate([extra_c[0, 1:2], extra_c[1, 1:2]], axis=1) + cross_b * slope_ii
     loss_ref[...] = jnp.broadcast_to(extra_c[0, 2:3, :128] + extra_c[1, 2:3, :128], (8, 128))
@@ -545,8 +567,7 @@
         frames, width = view_a.shape
         both, half = 2 * frames, width // 2
         quarter = half // 2
-        top = width // 2
-        rows_x, rows_z, rows_o = top // nx, top // nz, top // (nx * nz)
+        rows_x, rows_z, rows_o = width // nx, width // nz, width // (nx * nz)
         vmem = pltpu.VMEM
         rings = []
         scratch = [
@@ -580,8 +601,8 @@
         ring_y = [vmem((frames, half), bf16)] * 2 + [vmem((both, half), bf16)] * 2
         scratch += rings[0] + rings[1] + rings[0] + rings[1] + ring_y + ring_y + [
             vmem((frames, width), f32),
-            pltpu.SemaphoreType.DMA((256,)),
-            pltpu.SemaphoreType.DMA((256,)),
+            pltpu.SemaphoreType.DMA((160,)),
+            pltpu.SemaphoreType.DMA((160,)),
         ]
         grad_a, grad_b, loss = pl.pallas_call(
             functools.partial(kernel, nx, nz, ny, float(frames * members)),

time: 143 us -> 148 us (1.035)
  Pallas kernels: 138 us -> 143 us
    pallas_call x1, Pallas kernels: 138 us -> 143 us  [per_device(): pl.pallas_call(functools.partial(kernel, nx, nz, ny, float(frames * membe...]
where the time goes in v3:
time: 148 us
  Pallas kernels  143 us (97%)
  local copies, waits for them, and re-layouts  4.06 us (3%)
    pallas_call x1, Pallas kernels, per_device(): pl.pallas_call(functools.partial(kernel, nx, nz, ny, float(frames * membe...  143 us

profile of v3, /device:TPU:1, one launch (start us, length us, event | category | flops | bytes accessed | tf_op | source)
XLA Modules:
  0.0 148.0 jit_solution(11742652065569389747)
XLA Ops:
  0.6 143.3 %shard_map.49 = (bf16[320,1024]{1,0:T(8,128)(2,1)}, bf16[320,1024]{1,0:T(8,128)(2,1)}, f32[8,128]{1,0:T(8,128)}) custom-call(bf16[320,1024]{1,0:T(8,128)(2,1)} %a_ref.1, bf16[320,1024]{1,0:T(8,128)(2,1)} %b_ref.1), custom_call_target="tpu_custom_call" | custom-call | flops 8053063680 | bytes 2621440 | tf_op jit(solution)/shard_map/pallas_call | solution.py:607
  144.0 1.2 slice.3
  145.2 0.0 copy-start
  145.2 2.0 %copy.7 = bf16[320,1024]{1,0:T(8,128)(2,1)} copy(bf16[320,1024]{1,0:T(8,128)(2,1)} %get-tuple-element.12) | data formatting | bytes 1310720
  147.2 0.0 copy-done
  147.2 0.8 copy.8
Async XLA Ops:
  145.2 2.0 %copy-start = (bf16[320,1024]{1,0:T(8,128)(2,1)S(1)}, bf16[320,1024]{1,0:T(8,128)(2,1)}, u32[]{:S(2)}) copy-start(bf16[320,1024]{1,0:T(8,128)(2,1)} %get-tuple-element.13) | copy-start | bytes 1966084

commit v4 on v3

--- a/solution.py
+++ b/solution.py
@@ -14,7 +14,7 @@
 f32 = jnp.float32
 bf16 = jnp.bfloat16
 
-SHIFT = (0, 1, 3, 2)
+PIECES = ((0, 0), (0, 1), (1, 1), (2, 0), (3, 0), (3, 1), (1, 0), (2, 1))
 SLOT = (0, 1, 3, 2)
 
 
@@ -43,13 +43,13 @@
     mean_b16, square, extra_y, extra_c, extra_a, row_acc,
     rx_p1, rx_m1, rx_p2, rx_m2, rz_p1, rz_m1, rz_p2, rz_m2,
     sx_p1, sx_m1, sx_p2, sx_m2, sz_p1, sz_m1, sz_p2, sz_m2,
-    ry_p1, ry_m1, ry_p2, ry_m2, sy_p1, sy_m1, sy_p2, sy_m2, recv_a,
+    sy, ry, recv_a,
     send_sems, recv_sems,
 ):
     frames, width = a_ref.shape
     both = 2 * frames
     half = width // 2
-    slots = ny
+    slots, count, piece = ny, 2 * ny, half // 2
     dp = lax.axis_index("dp")
     m = lax.axis_index("mp")
     c = lax.rem(dp, 2)
@@ -123,6 +123,7 @@
         stat_c[c, 1, view : view + 1, :] = column_sum(deviation)
 
     pl.semaphore_wait(barrier, len(everyone))
+    work(5.0)
 
     def merge(buf, members, count):
         center = sum(buf[i, 0] for i in range(members)) * (1.0 / members)
@@ -152,14 +153,21 @@
         lax.fori_loop(0, frames // 32, body, 0)
 
     standardize(b_ref, nb16, center_b, inv_b)
-    swap_b = send(nb16.at[:, other_half], nb.at[0, other], partner)
-    nb[0, own, :] = nb16[:, own_half]
+    swap_b = [
+        send(
+            nb16.at[:, pl.ds(pl.multiple_of((1 - c) * half + side * piece, 128), piece)],
+            nb.at[side, other], partner)
+        for side in range(2)
+    ]
+    for side in range(2):
+        nb[side, own, :] = nb16[:, pl.ds(pl.multiple_of(c * half + side * piece, 128), piece)]
     up, down = device(dy=1), device(dy=ny - 1)
-    first = [send(nb.at[0, own], nb.at[2, own], up, "y+")]
+    first = [send(nb.at[0, own], nb.at[3, own], up, "y+"), send(nb.at[1, own], nb.at[2, own], down, "y-")]
     standardize(a_ref, na, center_a, inv_a)
     swap_a = send(na.at[own], na.at[other], partner)
-    arrive([swap_b])
-    first.append(send(nb.at[0, other], nb.at[1, other], down, "y-"))
+    arrive(swap_b)
+    first.append(send(nb.at[0, other], nb.at[3, other], up, "y+"))
+    first.append(send(nb.at[1, other], nb.at[2, other], down, "y-"))
 
     diag_done = []
 
@@ -192,15 +200,17 @@
         yield copies
         mean_a = jnp.concatenate([diag_f[0, 0, 0:1], diag_f[1, 0, 0:1]], axis=1)
         na[pl.ds(both, 16), :] = jnp.broadcast_to(mean_a, (16, width)).astype(bf16)
-        for p in range(slots):
-            nb[p, pl.ds(both, 16), :] = jnp.broadcast_to(mean_b16[p], (16, half)).astype(bf16)
+        for p, (slot, side) in enumerate(PIECES):
+            mean_b = mean_b16[slot, :, side * piece : (side + 1) * piece]
+            nb[p, pl.ds(both, 16), :] = jnp.broadcast_to(mean_b, (16, piece)).astype(bf16)
         diag_done.append(True)
 
-    def correlate(p):
+    def correlate(first):
         work(1.5)
         def body(i, _):
             rows = pl.ds(pl.multiple_of(i * 256, 256), 256)
-            part[p, rows, :] = jnp.dot(nat[rows, :], nb[p, :both, :], preferred_element_type=f32)
+            for p in (first, first + 1):
+                part[p, rows, :] = jnp.dot(nat[rows, :], nb[p, :both, :], preferred_element_type=f32)
             return 0
         lax.fori_loop(0, width // 256, body, 0)
 
@@ -301,8 +311,8 @@
         col_ids = lax.broadcasted_iota(jnp.int32, (rows_o, columns), 1) + (c * half + column)
         for p in range(first, first + count):
             value = 2.0 * off_weight * (part[p, rows, cols] / total)
-            if p == 0:
-                value = jnp.where(row_ids == col_ids, 0.0, value)
+            if p < 2:
+                value = jnp.where(row_ids == col_ids + p * piece, 0.0, value)
             slope[p, rows, cols] = value.astype(bf16)
 
     def one_way(group):
@@ -345,129 +355,115 @@
             if entry[3] is None:
                 live.remove(entry)
 
-    def group(rank, way, what, post):
-        def chain():
+    def group(rank, ways, first, post):
+        left = [len(ways)]
+        def chain(way, what):
             yield from way(what)
-            yield lambda: diag_done
-            yield from post
-        spawn(rank, chain())
-
-    def to_b(group):
-        first, count, column, columns = group
-        work(1.5 * count * columns / half)
-        for p in range(first, first + count):
-            def body(i, _, p=p):
-                cols = pl.ds(pl.multiple_of(column + i * 256, 256), 256)
-                part_b[p, :, cols] = jnp.dot(na[...], slope[p, :, cols], preferred_element_type=f32)
-                return 0
-            if columns == 256:
-                cols = pl.ds(column, 256)
-                part_b[p, :, cols] = jnp.dot(na[...], slope[p, :, cols], preferred_element_type=f32)
-            else:
-                lax.fori_loop(0, columns // 256, body, 0)
+            left[0] -= 1
+            if not left[0]:
+                yield lambda: diag_done
+                yield from post
+        for at, way in enumerate(ways):
+            pieces = 2 // len(ways)
+            spawn(rank, chain(way, (first + at * pieces, pieces, 0, piece)))
+
+    def to_b(first):
+        work(1.5)
+        for p in (first, first + 1):
+            part_b[p] = jnp.dot(na[...], slope[p], preferred_element_type=f32)
 
     begun = []
 
-    def to_a(group):
-        first, count, column, columns = group
-        cols = pl.ds(column, columns)
+    def to_a(first):
         fresh = not begun
-        work(0.5 + 1.5 * count * columns / half)
-        begun.append(group)
+        work(2.0)
+        begun.append(first)
         def body(i, _):
             rows = pl.ds(pl.multiple_of(i * 256, 256), 256)
             acc = None if fresh else back_a[:, rows]
-            for p in range(first, first + count):
+            for p in (first, first + 1):
                 term = lax.dot_general(
-                    nb[p, :, cols], slope[p, rows, cols], (((1,), (1,)), ((), ())),
-                    preferred_element_type=f32)
+                    nb[p], slope[p, rows, :], (((1,), (1,)), ((), ())), preferred_element_type=f32)
                 acc = term if acc is None else acc + term
             back_a[:, rows] = acc
             return 0
         lax.fori_loop(0, width // 256, body, 0)
 
-    def squares(group):
-        first, count, column, columns = group
-        work(0.6 * count * columns / half)
-        cols = pl.ds(column, columns)
-        for p in range(first, first + count):
+    def squares(first):
+        work(0.6)
+        for p in (first, first + 1):
             def body(i, acc, p=p):
-                rows = pl.ds(pl.multiple_of(i * 32, 32), 32)
-                s = slope[p, rows, cols].astype(f32)
+                rows = pl.ds(pl.multiple_of(i * 64, 64), 64)
+                s = slope[p, rows, :].astype(f32)
                 s = s * s
-                row_acc[rows, :] += sum(s[:, k * 128 : (k + 1) * 128] for k in range(columns // 128))
+                row_acc[rows, :] += sum(s[:, k * 128 : (k + 1) * 128] for k in range(piece // 128))
                 return acc + jnp.sum(s, axis=0, keepdims=True)
-            square[p, :, cols] = lax.fori_loop(0, width // 32, body, jnp.zeros((1, columns), f32))
-
-    far_ready, near_y = [], []
-
-    def wait_far(copies):
+            square[p] = lax.fori_loop(0, width // 64, body, jnp.zeros((1, piece), f32))
+
+    def code(out, base, extra):
+        work(0.5)
+        def body(i, _):
+            rows = pl.ds(pl.multiple_of(i * 64, 64), 64)
+            value = part_b[base, rows, :]
+            if extra is not None:
+                value = value + decode(ry[extra, rows, :])
+            sy[out, rows, :] = encode(value)
+            return 0
+        lax.fori_loop(0, both // 64, body, 0)
+
+    def gain(base, extra):
+        work(0.5)
+        def body(i, _):
+            rows = pl.ds(pl.multiple_of(i * 64, 64), 64)
+            part_b[base, rows, :] += decode(ry[extra, rows, :])
+            return 0
+        lax.fori_loop(0, both // 64, body, 0)
+
+    done, last_y = [], []
+
+    def post(first):
+        to_b(first)
+        if first:
+            copies = []
+            if first == 6:
+                yield lambda: "far" in done
+            for p, peer, link in ((first, up, "y+"), (first + 1, down, "y-")):
+                code(p - 2, p, p - 4 if first == 6 else None)
+                copies.append(send(sy.at[p - 2], ry.at[p - 2], peer, link))
+            if first == 6:
+                last_y.extend(copies)
+            else:
+                spawn(0, after_y(first, copies))
+            yield []
+        else:
+            done.append("own")
+        to_a(first)
+        squares(first)
+
+    def after_y(first, copies):
         yield copies
-        far_ready.append(True)
-
-    def post_own():
-        to_b(OWN)
-        to_a(OWN)
-        squares(OWN)
-        yield []
-
-    def post_far():
-        to_b(FAR)
-        work(1.0)
-        def body(i, _):
-            here = pl.ds(pl.multiple_of(i * 32, 32), 32)
-            there = pl.ds(pl.multiple_of(i * 32 + frames, 32), 32)
-            plus, minus = encode(part_b[3, here, :]), encode(part_b[3, there, :])
-            sy_p1[here, :] = plus
-            sy_m1[here, :] = minus
-            return 0
-        lax.fori_loop(0, frames // 32, body, 0)
-        spawn(0, wait_far([send(sy_p1, ry_p1, up, "y+"), send(sy_m1, ry_m1, down, "y-")]))
-        yield []
-        to_a(FAR)
-        squares(FAR)
-
-    def post_near(what, out, got, into, peer, link, near, rest):
-        to_b(what)
-        yield lambda: far_ready
-        work(1.0)
-        p = what[0]
-        def body(i, _):
-            here = pl.ds(pl.multiple_of(i * 32, 32), 32)
-            rows_n = pl.ds(pl.multiple_of(i * 32 + near, 32), 32)
-            rows_r = pl.ds(pl.multiple_of(i * 32 + rest, 32), 32)
-            first_half = encode(part_b[p, rows_n, :] + decode(got[here, :]))
-            other_part = encode(part_b[p, rows_r, :])
-            out[rows_n, :] = first_half
-            out[rows_r, :] = other_part
-            return 0
-        lax.fori_loop(0, frames // 32, body, 0)
-        near_y.append(send(out, into, peer, link))
-        yield []
-        to_a(what)
-        squares(what)
-
-    OWN, UP, DOWN, FAR = ((p, 1, 0, half) for p in range(slots))
+        if first == 4:
+            done.append("far")
+            return
+        yield lambda: "own" in done
+        gain(1, 0)
+        gain(0, 1)
 
     def blocks():
         yield first
-        second = [
-            send(nb.at[2, own], nb.at[3, own], up, "y+"),
-            send(nb.at[1, other], nb.at[3, other], down, "y-"),
-        ]
-        third = [
-            send(nb.at[0, other], nb.at[2, other], up, "y+"),
-            send(nb.at[0, own], nb.at[1, own], down, "y-"),
-        ]
+        second = [send(nb.at[3, :both], nb.at[4, :both], up, "y+"), send(nb.at[2, :both], nb.at[5, :both], down, "y-")]
+        third = [send(nb.at[1, :both], nb.at[7, :both], up, "y+"), send(nb.at[0, :both], nb.at[6, :both], down, "y-")]
+        correlate(2)
+        group(RANKS[1], WAYS[1], 2, post(2))
         yield second
-        correlate(3)
-        group(2, one_way, FAR, post_far())
+        correlate(4)
+        group(RANKS[2], WAYS[2], 4, post(4))
         yield third
-        correlate(1)
-        group(1, other_way, UP, post_near(UP, sy_p2, ry_p1, ry_p2, up, "y+", 0, frames))
-        yield []
-        correlate(2)
-        group(1, one_way, DOWN, post_near(DOWN, sy_m2, ry_m1, ry_m2, down, "y-", frames, 0))
+        correlate(6)
+        group(RANKS[3], WAYS[3], 6, post(6))
+
+    WAYS = [[one_way], [one_way], [other_way], [one_way]]
+    RANKS = [4, 3, 2, 1]
 
     row_acc[...] = jnp.zeros_like(row_acc)
     arrive([swap_a])
@@ -477,7 +473,7 @@
     work(2.0)
     correlate(0)
     spawn(0, blocks())
-    group(3, one_way, OWN, post_own())
+    group(RANKS[0], WAYS[0], 0, post(0))
     spawn(2, diagonal())
     run()
 
@@ -485,13 +481,16 @@
 
     scale = 1.0 / (2.0 * off_weight)
     corr_half = diag_f[c, 1, 0:1]
-    loss_off = jnp.sum(sum(square[p] for p in range(slots)), axis=1, keepdims=True)
+    loss_off = jnp.sum(sum(square[p] for p in range(count)), axis=1, keepdims=True)
     loss_diag = jnp.sum((1.0 - corr_half) ** 2, axis=1, keepdims=True)
     loss_row = jnp.broadcast_to(loss_off * (off_weight * scale * scale) + loss_diag, (1, half))
     for p in range(slots):
         block = extra_y.at[ny + p] if p else extra_y.at[m]
-        block[0:1, :] = part_b[p, both : both + 1, :]
-        block[1:2, :] = square[p] * scale
+        left, right = PIECES.index((p, 0)), PIECES.index((p, 1))
+        block[0:1, :piece] = part_b[left, both : both + 1, :]
+        block[0:1, piece:] = part_b[right, both : both + 1, :]
+        block[1:2, :piece] = square[left] * scale
+        block[1:2, piece:] = square[right] * scale
         block[2:3, :] = loss_row
         block[3:4, :] = jnp.zeros((1, half), f32)
     share_y = [
@@ -526,18 +525,22 @@
     extra_c[c] = sum(extra_y[i] for i in range(ny))
     share_c = send(extra_c.at[c], extra_c.at[c], partner)
 
-    def add_last(base):
-        def body(i, _):
-            rows = pl.ds(pl.multiple_of(base + i * 32, 32), 32)
-            sum_b[rows, :] = part_b[0, rows, :] + decode(ry_p2[rows, :]) + decode(ry_m2[rows, :])
-            return 0
-        lax.fori_loop(0, frames // 32, body, 0)
-
-    arrive(near_y)
-    add_last(frames)
-    swap_sum = [send(sum_b.at[other, :], full_b.at[:, own_half], partner)]
-    add_last(0)
-    full_b[:, own_half] = sum_b[own, :]
+    def add_last(base, dst, at):
+        for side, got in ((0, 4), (1, 5)):
+            cols = pl.ds(at if isinstance(at, int) else pl.multiple_of(at + side * piece, 128), piece)
+            if isinstance(at, int):
+                cols = pl.ds(side * piece, piece)
+            def body(i, _, side=side, got=got, cols=cols):
+                rows = pl.ds(pl.multiple_of(base + i * 64, 64), 64)
+                here = pl.ds(pl.multiple_of(i * 64, 64), 64)
+                dst[here, cols] = part_b[side, rows, :] + decode(ry[got, rows, :])
+                return 0
+            lax.fori_loop(0, frames // 64, body, 0)
+
+    arrive(last_y)
+    add_last(frames, sum_b, 0)
+    swap_sum = [send(sum_b, full_b.at[:, own_half], partner)]
+    add_last(0, full_b, c * half)
 
     arrive([share_c])
     mean_b = jnp.concatenate([extra_c[0, 0:1], extra_c[1, 0:1]], axis=1) + mean_a16 * slope_ii
@@ -566,20 +569,20 @@
     def per_device(view_a, view_b):
         frames, width = view_a.shape
         both, half = 2 * frames, width // 2
-        quarter = half // 2
         rows_x, rows_z, rows_o = width // nx, width // nz, width // (nx * nz)
         vmem = pltpu.VMEM
         rings = []
+        count, piece = 2 * ny, half // 2
         scratch = [
             vmem((frames, width), bf16),
             vmem((both + 16, width), bf16),
             vmem((width, both), bf16),
-            vmem((ny, both + 16, half), bf16),
-            vmem((ny, width, half), f32),
-            vmem((ny, width, half), bf16),
+            vmem((count, both + 16, piece), bf16),
+            vmem((count, width, piece), f32),
+            vmem((count, width, piece), bf16),
             vmem((both + 16, width), f32),
-            vmem((ny, both + 16, half), f32),
-            vmem((both, half), f32),
+            vmem((count, both + 16, piece), f32),
+            vmem((frames, half), f32),
             vmem((frames, width), f32),
             vmem((2, 2, 2, width), f32),
             vmem((nx, 2, 2, width), f32),
@@ -589,20 +592,19 @@
             vmem((nz, 3, 2, half), f32),
             vmem((2, 3, 2, half), f32),
             vmem((ny, 1, half), f32),
-            vmem((ny, 1, half), f32),
+            vmem((count, 1, piece), f32),
             vmem((2 * ny, 4, half), f32),
             vmem((2, 4, half), f32),
             vmem((2, 2, width), f32),
             vmem((width, 128), f32),
         ]
         for rows, n in ((rows_x + rows_o, nx), (rows_z + rows_o, nz)):
-            ring = [vmem((ny, rows, quarter), bf16)] * 2 + [vmem((n // 2 - 1, ny, rows, half), bf16)] * 2
-            rings.append(ring)
-        ring_y = [vmem((frames, half), bf16)] * 2 + [vmem((both, half), bf16)] * 2
-        scratch += rings[0] + rings[1] + rings[0] + rings[1] + ring_y + ring_y + [
+            ring = [vmem((count, rows, piece // 2), bf16)] * 2
+            rings.append(ring + [vmem((n // 2 - 1, count, rows, piece), bf16)] * 2)
+        scratch += rings[0] + rings[1] + rings[0] + rings[1] + [vmem((count - 2, both, piece), bf16)] * 2 + [
             vmem((frames, width), f32),
-            pltpu.SemaphoreType.DMA((160,)),
-            pltpu.SemaphoreType.DMA((160,)),
+            pltpu.SemaphoreType.DMA((256,)),
+            pltpu.SemaphoreType.DMA((256,)),
         ]
         grad_a, grad_b, loss = pl.pallas_call(
             functools.partial(kernel, nx, nz, ny, float(frames * members)),

time: 148 us -> 133 us (0.90)
  Pallas kernels: 143 us -> 128 us
    pallas_call x1, Pallas kernels: 143 us -> 128 us  [per_device(): pl.pallas_call(functools.partial(kernel, nx, nz, ny, float(frames * membe...]
where the time goes in v4:
time: 133 us
  Pallas kernels  128 us (96%)
  local copies, waits for them, and re-layouts  4.06 us (3%)
    pallas_call x1, Pallas kernels, per_device(): pl.pallas_call(functools.partial(kernel, nx, nz, ny, float(frames * membe...  128 us
    unnamed x4, local copies, waits for them, and re-layouts  2.87 us

profile of v4, /device:TPU:1, one launch (start us, length us, event | category | flops | bytes accessed | tf_op | source)
XLA Modules:
  0.0 132.7 jit_solution(5701667063168366135)
XLA Ops:
  0.6 128.0 %shard_map.49 = (bf16[320,1024]{1,0:T(8,128)(2,1)}, bf16[320,1024]{1,0:T(8,128)(2,1)}, f32[8,128]{1,0:T(8,128)}) custom-call(bf16[320,1024]{1,0:T(8,128)(2,1)} %a_ref.1, bf16[320,1024]{1,0:T(8,128)(2,1)} %b_ref.1), custom_call_target="tpu_custom_call" | custom-call | flops 8053063680 | bytes 2621440 | tf_op jit(solution)/shard_map/pallas_call | solution.py:609
  128.6 1.2 slice.3
  129.8 0.0 copy-start
  129.8 2.0 %copy.7 = bf16[320,1024]{1,0:T(8,128)(2,1)} copy(bf16[320,1024]{1,0:T(8,128)(2,1)} %get-tuple-element.12) | data formatting | bytes 1310720
  131.9 0.0 copy-done
  131.9 0.8 copy.8
Async XLA Ops:
  129.8 2.0 %copy-start = (bf16[320,1024]{1,0:T(8,128)(2,1)S(1)}, bf16[320,1024]{1,0:T(8,128)(2,1)}, u32[]{:S(2)}) copy-start(bf16[320,1024]{1,0:T(8,128)(2,1)} %get-tuple-element.13) | copy-start | bytes 1966084

commit v5 on v4

--- a/solution.py
+++ b/solution.py
@@ -38,8 +38,8 @@
 def kernel(
     nx, nz, ny, total,
     a_ref, b_ref, ga_ref, gb_ref, loss_ref,
-    nb16, na, nat, nb, part, slope, back_a, part_b, sum_b, full_b,
-    stat_c, stat_x, stat_z, diag_c, diag_x, diag_z, diag_f,
+    nb16, na, nat, raw_a, raw_b, nb, part, slope, back_a, part_b, sum_b, full_b,
+    stat_x, stat_z, stat_y, diag_c, diag_x, diag_z, diag_f,
     mean_b16, square, extra_y, extra_c, extra_a, row_acc,
     rx_p1, rx_m1, rx_p2, rx_m2, rz_p1, rz_m1, rz_p2, rz_m2,
     sx_p1, sx_m1, sx_p2, sx_m2, sz_p1, sz_m1, sz_p2, sz_m2,
@@ -65,7 +65,8 @@
     peers_x = [device(dx=k) for k in range(1, nx)]
     peers_z = [device(dz=k) for k in range(1, nz)]
     peers_y = [device(dy=k) for k in range(1, ny)]
-    everyone = [partner] + peers_x + peers_z + peers_y
+    peers_cx = [device(dc=k % 2, dx=k // 2) for k in range(1, 2 * nx)]
+    everyone = peers_cx + peers_z + peers_y
 
     barrier = pltpu.get_barrier_semaphore()
     for peer in everyone:
@@ -108,22 +109,36 @@
     def spread_to(buf, mine, peers):
         return [send(buf.at[mine], buf.at[mine], peer) for peer in peers]
 
+    own, other = pl.ds(0, frames), pl.ds(frames, frames)
+    own_half = pl.ds(pl.multiple_of(c * half, 128), half)
+    up, down = device(dy=1), device(dy=ny - 1)
+
+    def piece_of(core, side):
+        return pl.ds(pl.multiple_of(core * half + side * piece, 128), piece)
+
+    for side in range(2):
+        raw_b[side, own, :] = b_ref[:, piece_of(c, side)]
+    pl.semaphore_wait(barrier, len(everyone))
+    work(3.0)
+    first = [send(raw_b.at[0, own], raw_b.at[3, own], up, "y+"), send(raw_b.at[1, own], raw_b.at[2, own], down, "y-")]
+    swap_b = [send(b_ref.at[:, piece_of(1 - c, side)], raw_b.at[side, other], partner) for side in range(2)]
+    swap_a = send(a_ref, raw_a, partner)
+
     def column_sum(fn):
         step = 64
         def body(i, acc):
             return acc + jnp.sum(fn(pl.ds(i * step, step)), axis=0, keepdims=True)
         return lax.fori_loop(0, frames // step, body, jnp.zeros((1, width), f32))
 
+    at_cx = 2 * x + c
     for view, ref in enumerate((a_ref, b_ref)):
         center = column_sum(lambda rows: ref[rows, :].astype(f32)) / frames
         def deviation(rows, ref=ref, center=center):
             dev = ref[rows, :].astype(f32) - center
             return dev * dev
-        stat_c[c, 0, view : view + 1, :] = center
-        stat_c[c, 1, view : view + 1, :] = column_sum(deviation)
-
-    pl.semaphore_wait(barrier, len(everyone))
-    work(5.0)
+        stat_x[at_cx, 0, view : view + 1, :] = center
+        stat_x[at_cx, 1, view : view + 1, :] = column_sum(deviation)
+    work(2.0)
 
     def merge(buf, members, count):
         center = sum(buf[i, 0] for i in range(members)) * (1.0 / members)
@@ -131,47 +146,52 @@
         shift = sum((buf[i, 0] - center) ** 2 for i in range(members))
         return center, spread + count * shift
 
-    arrive(spread_to(stat_c, c, [partner]))
-    stat_x[x, 0], stat_x[x, 1] = merge(stat_c, 2, float(frames))
-    arrive(spread_to(stat_x, x, peers_x))
-    stat_z[z, 0], stat_z[z, 1] = merge(stat_x, nx, float(frames * 2))
-    arrive(spread_to(stat_z, z, peers_z))
+    copies = spread_to(stat_x, at_cx, peers_cx)
+    arrive(swap_b)
+    first.append(send(raw_b.at[0, other], raw_b.at[3, other], up, "y+"))
+    first.append(send(raw_b.at[1, other], raw_b.at[2, other], down, "y-"))
+    arrive(copies)
+    stat_z[z, 0], stat_z[z, 1] = merge(stat_x, 2 * nx, float(frames))
+    copies = spread_to(stat_z, z, peers_z)
+    arrive(first)
+    second = [send(raw_b.at[3], raw_b.at[4], up, "y+"), send(raw_b.at[2], raw_b.at[5], down, "y-")]
+    third = [send(raw_b.at[1], raw_b.at[7], up, "y+"), send(raw_b.at[0], raw_b.at[6], down, "y-")]
+    arrive(copies)
     center, spread = merge(stat_z, nz, float(frames * 2 * nx))
     inv = lax.rsqrt(spread / total + epsilon)
     center_a, center_b = center[0:1], center[1:2]
     inv_a, inv_b = inv[0:1], inv[1:2]
-
-    own, other = pl.ds(0, frames), pl.ds(frames, frames)
-    own_half = pl.ds(pl.multiple_of(c * half, 128), half)
-    other_half = pl.ds(pl.multiple_of((1 - c) * half, 128), half)
-
-    def standardize(src, dst, center, inv):
+    stat_y[0, 0:1, :] = jnp.where(c == 0, center_b[:, :half], center_b[:, half:])
+    stat_y[0, 1:2, :] = jnp.where(c == 0, inv_b[:, :half], inv_b[:, half:])
+    share_stat = [send(stat_y.at[0], stat_y.at[SLOT[ny - k]], peers_y[k - 1]) for k in range(1, ny)]
+
+    def standardize(src, src_at, dst, dst_at, base, step, center, inv):
         def body(i, _):
-            rows = pl.ds(pl.multiple_of(i * 32, 32), 32)
-            dst[rows, :] = ((src[rows, :].astype(f32) - center) * inv).astype(bf16)
+            rows = pl.ds(pl.multiple_of(i * step, 32), step)
+            there = pl.ds(pl.multiple_of(base + i * step, 32), step)
+            dst[(*dst_at, there, slice(None))] = (
+                (src[(*src_at, rows, slice(None))].astype(f32) - center) * inv
+            ).astype(bf16)
             return 0
-        lax.fori_loop(0, frames // 32, body, 0)
-
-    standardize(b_ref, nb16, center_b, inv_b)
-    swap_b = [
-        send(
-            nb16.at[:, pl.ds(pl.multiple_of((1 - c) * half + side * piece, 128), piece)],
-            nb.at[side, other], partner)
-        for side in range(2)
-    ]
-    for side in range(2):
-        nb[side, own, :] = nb16[:, pl.ds(pl.multiple_of(c * half + side * piece, 128), piece)]
-    up, down = device(dy=1), device(dy=ny - 1)
-    first = [send(nb.at[0, own], nb.at[3, own], up, "y+"), send(nb.at[1, own], nb.at[2, own], down, "y-")]
-    standardize(a_ref, na, center_a, inv_a)
-    swap_a = send(na.at[own], na.at[other], partner)
-    arrive(swap_b)
-    first.append(send(nb.at[0, other], nb.at[3, other], up, "y+"))
-    first.append(send(nb.at[1, other], nb.at[2, other], down, "y-"))
+        return body
+
+    def pieces_in(first):
+        work(0.4)
+        for p in (first, first + 1):
+            slot, side = PIECES[p]
+            cols = slice(side * piece, (side + 1) * piece)
+            body = standardize(raw_b, (p,), nb, (p,), 0, 64, stat_y[slot, 0:1, cols], stat_y[slot, 1:2, cols])
+            lax.fori_loop(0, both // 64, body, 0)
+
+    lax.fori_loop(0, frames // 32, standardize(a_ref, (), na, (), 0, 32, center_a, inv_a), 0)
+    arrive([swap_a])
+    lax.fori_loop(0, frames // 32, standardize(raw_a, (), na, (), frames, 32, center_a, inv_a), 0)
+    pieces_in(0)
 
     diag_done = []
 
     def diagonal():
+        lax.fori_loop(0, frames // 32, standardize(b_ref, (), nb16, (), 0, 32, center_b, inv_b), 0)
         def body(i, acc):
             rows = pl.ds(pl.multiple_of(i * 32, 32), 32)
             wide_a = (a_ref[rows, :].astype(f32) - center_a) * inv_a
@@ -367,10 +387,9 @@
             pieces = 2 // len(ways)
             spawn(rank, chain(way, (first + at * pieces, pieces, 0, piece)))
 
-    def to_b(first):
-        work(1.5)
-        for p in (first, first + 1):
-            part_b[p] = jnp.dot(na[...], slope[p], preferred_element_type=f32)
+    def to_b(p):
+        work(0.75)
+        part_b[p] = jnp.dot(na[...], slope[p], preferred_element_type=f32)
 
     begun = []
 
@@ -422,12 +441,12 @@
     done, last_y = [], []
 
     def post(first):
-        to_b(first)
         if first:
             copies = []
             if first == 6:
                 yield lambda: "far" in done
             for p, peer, link in ((first, up, "y+"), (first + 1, down, "y-")):
+                to_b(p)
                 code(p - 2, p, p - 4 if first == 6 else None)
                 copies.append(send(sy.at[p - 2], ry.at[p - 2], peer, link))
             if first == 6:
@@ -436,6 +455,8 @@
                 spawn(0, after_y(first, copies))
             yield []
         else:
+            to_b(0)
+            to_b(1)
             done.append("own")
         to_a(first)
         squares(first)
@@ -450,15 +471,16 @@
         gain(0, 1)
 
     def blocks():
-        yield first
-        second = [send(nb.at[3, :both], nb.at[4, :both], up, "y+"), send(nb.at[2, :both], nb.at[5, :both], down, "y-")]
-        third = [send(nb.at[1, :both], nb.at[7, :both], up, "y+"), send(nb.at[0, :both], nb.at[6, :both], down, "y-")]
+        yield share_stat
+        pieces_in(2)
         correlate(2)
         group(RANKS[1], WAYS[1], 2, post(2))
         yield second
+        pieces_in(4)
         correlate(4)
         group(RANKS[2], WAYS[2], 4, post(4))
         yield third
+        pieces_in(6)
         correlate(6)
         group(RANKS[3], WAYS[3], 6, post(6))
 
@@ -466,7 +488,6 @@
     RANKS = [4, 3, 2, 1]
 
     row_acc[...] = jnp.zeros_like(row_acc)
-    arrive([swap_a])
     for i in range(width // 128):
         cols = pl.ds(i * 128, 128)
         nat[cols, :] = jnp.transpose(na[:both, cols].astype(f32)).astype(bf16)
@@ -577,6 +598,8 @@
             vmem((frames, width), bf16),
             vmem((both + 16, width), bf16),
             vmem((width, both), bf16),
+            vmem((frames, width), bf16),
+            vmem((count, both, piece), bf16),
             vmem((count, both + 16, piece), bf16),
             vmem((count, width, piece), f32),
             vmem((count, width, piece), bf16),
@@ -584,9 +607,9 @@
             vmem((count, both + 16, piece), f32),
             vmem((frames, half), f32),
             vmem((frames, width), f32),
-            vmem((2, 2, 2, width), f32),
-            vmem((nx, 2, 2, width), f32),
+            vmem((2 * nx, 2, 2, width), f32),
             vmem((nz, 2, 2, width), f32),
+            vmem((ny, 2, half), f32),
             vmem((2, 3, 2, width), f32),
             vmem((nx, 3, 2, half), f32),
             vmem((nz, 3, 2, half), f32),

time: 133 us -> 140 us (1.053)
  Pallas kernels: 128 us -> 135 us
    pallas_call x1, Pallas kernels: 128 us -> 135 us  [per_device(): pl.pallas_call(functools.partial(kernel, nx, nz, ny, float(frames * membe...]
where the time goes in v5:
time: 140 us
  Pallas kernels  135 us (96%)
  local copies, waits for them, and re-layouts  4.06 us (3%)
    pallas_call x1, Pallas kernels, per_device(): pl.pallas_call(functools.partial(kernel, nx, nz, ny, float(frames * membe...  135 us
    unnamed x4, local copies, waits for them, and re-layouts  2.87 us

profile of v5, /device:TPU:1, one launch (start us, length us, event | category | flops | bytes accessed | tf_op | source)
XLA Modules:
  0.0 139.8 jit_solution(2161237046640380336)
XLA Ops:
  0.6 135.1 %shard_map.49 = (bf16[320,1024]{1,0:T(8,128)(2,1)}, bf16[320,1024]{1,0:T(8,128)(2,1)}, f32[8,128]{1,0:T(8,128)}) custom-call(bf16[320,1024]{1,0:T(8,128)(2,1)} %a_ref.1, bf16[320,1024]{1,0:T(8,128)(2,1)} %b_ref.1), custom_call_target="tpu_custom_call" | custom-call | flops 8053063680 | bytes 2621440 | tf_op jit(solution)/shard_map/pallas_call | solution.py:632
  135.8 1.2 slice.3
  137.0 0.0 copy-start
  137.0 2.0 %copy.7 = bf16[320,1024]{1,0:T(8,128)(2,1)} copy(bf16[320,1024]{1,0:T(8,128)(2,1)} %get-tuple-element.12) | data formatting | bytes 1310720
  139.0 0.0 copy-done
  139.0 0.8 copy.8
Async XLA Ops:
  137.0 2.0 %copy-start = (bf16[320,1024]{1,0:T(8,128)(2,1)S(1)}, bf16[320,1024]{1,0:T(8,128)(2,1)}, u32[]{:S(2)}) copy-start(bf16[320,1024]{1,0:T(8,128)(2,1)} %get-tuple-element.13) | copy-start | bytes 1966084

commit v6 on v5

--- a/solution.py
+++ b/solution.py
@@ -22,17 +22,13 @@
 
 
 def encode(v):
-    q = v * v
-    q = q * q
-    return jnp.where(v < 0.0, -q, q).astype(bf16)
+    return ((v * v) * (v * jnp.abs(v))).astype(bf16)
 
 
 def decode(y):
     y = y.astype(f32)
-    q = jnp.abs(y)
-    q = q * lax.rsqrt(jnp.maximum(q, tiny))
-    q = q * lax.rsqrt(jnp.maximum(q, tiny))
-    return jnp.where(y < 0.0, -q, q)
+    y = y * lax.rsqrt(jnp.maximum(jnp.abs(y), tiny))
+    return y * lax.rsqrt(jnp.maximum(jnp.abs(y), tiny))
 
 
 def kernel(
@@ -72,7 +68,7 @@
     for peer in everyone:
         pl.semaphore_signal(barrier, inc=1, device_id=peer, device_id_type=MESH)
 
-    started, due, clock, free = [], {}, [0.0], {}
+    started, waited, due, clock, free = [], [], {}, [0.0], {}
 
     def work(t):
         clock[0] += t
@@ -104,7 +100,8 @@
     def arrive(copies):
         for copy in copies:
             clock[0] = max(clock[0], due[id(copy)])
-            copy.wait_recv()
+            copy.wait()
+            waited.append(id(copy))
 
     def spread_to(buf, mine, peers):
         return [send(buf.at[mine], buf.at[mine], peer) for peer in peers]
@@ -381,15 +378,24 @@
             yield from way(what)
             left[0] -= 1
             if not left[0]:
-                yield lambda: diag_done
+                if not diag_done:
+                    yield lambda: diag_done
                 yield from post
         for at, way in enumerate(ways):
             pieces = 2 // len(ways)
             spawn(rank, chain(way, (first + at * pieces, pieces, 0, piece)))
 
-    def to_b(p):
-        work(0.75)
-        part_b[p] = jnp.dot(na[...], slope[p], preferred_element_type=f32)
+    def to_b(p, extra=None):
+        work(1.0)
+        value = jnp.dot(na[...], slope[p], preferred_element_type=f32)
+        if p < 2:
+            part_b[p] = value
+            return
+        part_b[p, both:, :] = value[both:]
+        value = value[:both]
+        if extra is not None:
+            value = value + decode(ry[extra])
+        sy[p - 2] = encode(value)
 
     begun = []
 
@@ -397,38 +403,27 @@
         fresh = not begun
         work(2.0)
         begun.append(first)
-        def body(i, _):
+        pair = (first, first + 1)
+        def body(i, sums):
             rows = pl.ds(pl.multiple_of(i * 256, 256), 256)
             acc = None if fresh else back_a[:, rows]
-            for p in (first, first + 1):
+            for p in pair:
                 term = lax.dot_general(
                     nb[p], slope[p, rows, :], (((1,), (1,)), ((), ())), preferred_element_type=f32)
                 acc = term if acc is None else acc + term
             back_a[:, rows] = acc
-            return 0
-        lax.fori_loop(0, width // 256, body, 0)
-
-    def squares(first):
-        work(0.6)
-        for p in (first, first + 1):
-            def body(i, acc, p=p):
-                rows = pl.ds(pl.multiple_of(i * 64, 64), 64)
-                s = slope[p, rows, :].astype(f32)
-                s = s * s
-                row_acc[rows, :] += sum(s[:, k * 128 : (k + 1) * 128] for k in range(piece // 128))
-                return acc + jnp.sum(s, axis=0, keepdims=True)
-            square[p] = lax.fori_loop(0, width // 64, body, jnp.zeros((1, piece), f32))
-
-    def code(out, base, extra):
-        work(0.5)
-        def body(i, _):
-            rows = pl.ds(pl.multiple_of(i * 64, 64), 64)
-            value = part_b[base, rows, :]
-            if extra is not None:
-                value = value + decode(ry[extra, rows, :])
-            sy[out, rows, :] = encode(value)
-            return 0
-        lax.fori_loop(0, both // 64, body, 0)
+            over, new = None, []
+            for p, total_p in zip(pair, sums):
+                sq = slope[p, rows, :].astype(f32)
+                sq = sq * sq
+                lanes = sum(sq[:, k * 128 : (k + 1) * 128] for k in range(piece // 128))
+                over = lanes if over is None else over + lanes
+                new.append(total_p + jnp.sum(sq, axis=0, keepdims=True))
+            row_acc[rows, :] = over if fresh else row_acc[rows, :] + over
+            return tuple(new)
+        sums = lax.fori_loop(0, width // 256, body, (jnp.zeros((1, piece), f32),) * 2)
+        for p, value in zip(pair, sums):
+            square[p] = value
 
     def gain(base, extra):
         work(0.5)
@@ -446,8 +441,7 @@
             if first == 6:
                 yield lambda: "far" in done
             for p, peer, link in ((first, up, "y+"), (first + 1, down, "y-")):
-                to_b(p)
-                code(p - 2, p, p - 4 if first == 6 else None)
+                to_b(p, p - 4 if first == 6 else None)
                 copies.append(send(sy.at[p - 2], ry.at[p - 2], peer, link))
             if first == 6:
                 last_y.extend(copies)
@@ -459,7 +453,6 @@
             to_b(1)
             done.append("own")
         to_a(first)
-        squares(first)
 
     def after_y(first, copies):
         yield copies
@@ -487,15 +480,16 @@
     WAYS = [[one_way], [one_way], [other_way], [one_way]]
     RANKS = [4, 3, 2, 1]
 
-    row_acc[...] = jnp.zeros_like(row_acc)
     for i in range(width // 128):
         cols = pl.ds(i * 128, 128)
-        nat[cols, :] = jnp.transpose(na[:both, cols].astype(f32)).astype(bf16)
+        nat[cols, :] = jnp.transpose(na[:both, cols])
     work(2.0)
     correlate(0)
+    group(RANKS[0], WAYS[0], 0, post(0))
+    for entry in live:
+        entry[3] = next(entry[2])
     spawn(0, blocks())
-    group(RANKS[0], WAYS[0], 0, post(0))
-    spawn(2, diagonal())
+    spawn(1, diagonal())
     run()
 
     swap_back = send(back_a.at[other, :], recv_a, partner)
@@ -577,8 +571,7 @@
         return 0
 
     lax.fori_loop(0, frames // 32, finish_b, 0)
-    for copy in started:
-        copy.wait_send()
+    arrive([copy for copy in started if id(copy) not in waited])
 
 
 def solution(mesh):

time: 140 us -> 140 us (level)
  no operation moved by 1% of the time
where the time goes in v6:
time: 140 us
  Pallas kernels  135 us (96%)
  local copies, waits for them, and re-layouts  4.06 us (3%)
    pallas_call x1, Pallas kernels, per_device(): pl.pallas_call(functools.partial(kernel, nx, nz, ny, float(frames * membe...  135 us
    unnamed x4, local copies, waits for them, and re-layouts  2.87 us

profile of v6, /device:TPU:1, one launch (start us, length us, event | category | flops | bytes accessed | tf_op | source)
XLA Modules:
  0.0 139.8 jit_solution(4123487576068382050)
XLA Ops:
  0.6 135.1 %shard_map.49 = (bf16[320,1024]{1,0:T(8,128)(2,1)}, bf16[320,1024]{1,0:T(8,128)(2,1)}, f32[8,128]{1,0:T(8,128)}) custom-call(bf16[320,1024]{1,0:T(8,128)(2,1)} %a_ref.1, bf16[320,1024]{1,0:T(8,128)(2,1)} %b_ref.1), custom_call_target="tpu_custom_call" | custom-call | flops 8053063680 | bytes 2621440 | tf_op jit(solution)/shard_map/pallas_call | solution.py:625
  135.7 1.2 slice.3
  136.9 0.0 copy-start
  136.9 2.0 %copy.7 = bf16[320,1024]{1,0:T(8,128)(2,1)} copy(bf16[320,1024]{1,0:T(8,128)(2,1)} %get-tuple-element.12) | data formatting | bytes 1310720
  138.9 0.0 copy-done
  138.9 0.8 copy.8
Async XLA Ops:
  136.9 2.0 %copy-start = (bf16[320,1024]{1,0:T(8,128)(2,1)S(1)}, bf16[320,1024]{1,0:T(8,128)(2,1)}, u32[]{:S(2)}) copy-start(bf16[320,1024]{1,0:T(8,128)(2,1)} %get-tuple-element.13) | copy-start | bytes 1966084

commit v7 on v6

--- a/solution.py
+++ b/solution.py
@@ -35,11 +35,11 @@
     nx, nz, ny, total,
     a_ref, b_ref, ga_ref, gb_ref, loss_ref,
     nb16, na, nat, raw_a, raw_b, nb, part, slope, back_a, part_b, sum_b, full_b,
-    stat_x, stat_z, stat_y, diag_c, diag_x, diag_z, diag_f,
+    stat_c, stat_x, stat_z, diag_c, diag_x, diag_z, diag_f,
     mean_b16, square, extra_y, extra_c, extra_a, row_acc,
     rx_p1, rx_m1, rx_p2, rx_m2, rz_p1, rz_m1, rz_p2, rz_m2,
     sx_p1, sx_m1, sx_p2, sx_m2, sz_p1, sz_m1, sz_p2, sz_m2,
-    sy, ry, recv_a,
+    sy, ry, send_a, recv_a, recv_b,
     send_sems, recv_sems,
 ):
     frames, width = a_ref.shape
@@ -61,8 +61,7 @@
     peers_x = [device(dx=k) for k in range(1, nx)]
     peers_z = [device(dz=k) for k in range(1, nz)]
     peers_y = [device(dy=k) for k in range(1, ny)]
-    peers_cx = [device(dc=k % 2, dx=k // 2) for k in range(1, 2 * nx)]
-    everyone = peers_cx + peers_z + peers_y
+    everyone = [partner] + peers_x + peers_z + peers_y
 
     barrier = pltpu.get_barrier_semaphore()
     for peer in everyone:
@@ -107,19 +106,10 @@
         return [send(buf.at[mine], buf.at[mine], peer) for peer in peers]
 
     own, other = pl.ds(0, frames), pl.ds(frames, frames)
-    own_half = pl.ds(pl.multiple_of(c * half, 128), half)
     up, down = device(dy=1), device(dy=ny - 1)
 
     def piece_of(core, side):
         return pl.ds(pl.multiple_of(core * half + side * piece, 128), piece)
-
-    for side in range(2):
-        raw_b[side, own, :] = b_ref[:, piece_of(c, side)]
-    pl.semaphore_wait(barrier, len(everyone))
-    work(3.0)
-    first = [send(raw_b.at[0, own], raw_b.at[3, own], up, "y+"), send(raw_b.at[1, own], raw_b.at[2, own], down, "y-")]
-    swap_b = [send(b_ref.at[:, piece_of(1 - c, side)], raw_b.at[side, other], partner) for side in range(2)]
-    swap_a = send(a_ref, raw_a, partner)
 
     def column_sum(fn):
         step = 64
@@ -127,15 +117,16 @@
             return acc + jnp.sum(fn(pl.ds(i * step, step)), axis=0, keepdims=True)
         return lax.fori_loop(0, frames // step, body, jnp.zeros((1, width), f32))
 
-    at_cx = 2 * x + c
     for view, ref in enumerate((a_ref, b_ref)):
         center = column_sum(lambda rows: ref[rows, :].astype(f32)) / frames
         def deviation(rows, ref=ref, center=center):
             dev = ref[rows, :].astype(f32) - center
             return dev * dev
-        stat_x[at_cx, 0, view : view + 1, :] = center
-        stat_x[at_cx, 1, view : view + 1, :] = column_sum(deviation)
+        stat_c[c, 0, view : view + 1, :] = center
+        stat_c[c, 1, view : view + 1, :] = column_sum(deviation)
     work(2.0)
+    pl.semaphore_wait(barrier, len(everyone))
+    work(3.0)
 
     def merge(buf, members, count):
         center = sum(buf[i, 0] for i in range(members)) * (1.0 / members)
@@ -143,25 +134,18 @@
         shift = sum((buf[i, 0] - center) ** 2 for i in range(members))
         return center, spread + count * shift
 
-    copies = spread_to(stat_x, at_cx, peers_cx)
-    arrive(swap_b)
-    first.append(send(raw_b.at[0, other], raw_b.at[3, other], up, "y+"))
-    first.append(send(raw_b.at[1, other], raw_b.at[2, other], down, "y-"))
-    arrive(copies)
-    stat_z[z, 0], stat_z[z, 1] = merge(stat_x, 2 * nx, float(frames))
+    arrive(spread_to(stat_c, c, [partner]))
+    stat_x[x, 0], stat_x[x, 1] = merge(stat_c, 2, float(frames))
+    arrive(spread_to(stat_x, x, peers_x))
+    stat_z[z, 0], stat_z[z, 1] = merge(stat_x, nx, float(frames * 2))
     copies = spread_to(stat_z, z, peers_z)
-    arrive(first)
-    second = [send(raw_b.at[3], raw_b.at[4], up, "y+"), send(raw_b.at[2], raw_b.at[5], down, "y-")]
-    third = [send(raw_b.at[1], raw_b.at[7], up, "y+"), send(raw_b.at[0], raw_b.at[6], down, "y-")]
+    swap_b = [send(b_ref.at[:, piece_of(1 - c, side)], raw_b.at[side], partner) for side in range(2)]
+    swap_a = send(a_ref, raw_a, partner)
     arrive(copies)
     center, spread = merge(stat_z, nz, float(frames * 2 * nx))
     inv = lax.rsqrt(spread / total + epsilon)
     center_a, center_b = center[0:1], center[1:2]
     inv_a, inv_b = inv[0:1], inv[1:2]
-    stat_y[0, 0:1, :] = jnp.where(c == 0, center_b[:, :half], center_b[:, half:])
-    stat_y[0, 1:2, :] = jnp.where(c == 0, inv_b[:, :half], inv_b[:, half:])
-    share_stat = [send(stat_y.at[0], stat_y.at[SLOT[ny - k]], peers_y[k - 1]) for k in range(1, ny)]
-
     def standardize(src, src_at, dst, dst_at, base, step, center, inv):
         def body(i, _):
             rows = pl.ds(pl.multiple_of(i * step, 32), step)
@@ -172,23 +156,27 @@
             return 0
         return body
 
-    def pieces_in(first):
-        work(0.4)
-        for p in (first, first + 1):
-            slot, side = PIECES[p]
-            cols = slice(side * piece, (side + 1) * piece)
-            body = standardize(raw_b, (p,), nb, (p,), 0, 64, stat_y[slot, 0:1, cols], stat_y[slot, 1:2, cols])
-            lax.fori_loop(0, both // 64, body, 0)
-
+    def pick(row):
+        return jnp.where(c == 0, row[:, :half], row[:, half:])
+
+    center_h, inv_h = pick(center_b), pick(inv_b)
+    lax.fori_loop(0, frames // 32, standardize(b_ref, (), nb16, (), 0, 32, center_b, inv_b), 0)
+    for side in range(2):
+        nb[side, own, :] = nb16[:, piece_of(c, side)]
+    arrive(swap_b)
+    first = []
+    for side, at, peer, link in ((0, 3, up, "y+"), (1, 2, down, "y-")):
+        cols = slice(side * piece, (side + 1) * piece)
+        body = standardize(raw_b, (side,), nb, (side,), frames, 64, center_h[:, cols], inv_h[:, cols])
+        lax.fori_loop(0, frames // 64, body, 0)
+        first.append(send(nb.at[side, :both], nb.at[at, :both], peer, link))
     lax.fori_loop(0, frames // 32, standardize(a_ref, (), na, (), 0, 32, center_a, inv_a), 0)
     arrive([swap_a])
     lax.fori_loop(0, frames // 32, standardize(raw_a, (), na, (), frames, 32, center_a, inv_a), 0)
-    pieces_in(0)
 
     diag_done = []
 
     def diagonal():
-        lax.fori_loop(0, frames // 32, standardize(b_ref, (), nb16, (), 0, 32, center_b, inv_b), 0)
         def body(i, acc):
             rows = pl.ds(pl.multiple_of(i * 32, 32), 32)
             wide_a = (a_ref[rows, :].astype(f32) - center_a) * inv_a
@@ -464,16 +452,15 @@
         gain(0, 1)
 
     def blocks():
-        yield share_stat
-        pieces_in(2)
+        yield first
+        second = [send(nb.at[3, :both], nb.at[4, :both], up, "y+"), send(nb.at[2, :both], nb.at[5, :both], down, "y-")]
+        third = [send(nb.at[1, :both], nb.at[7, :both], up, "y+"), send(nb.at[0, :both], nb.at[6, :both], down, "y-")]
         correlate(2)
         group(RANKS[1], WAYS[1], 2, post(2))
         yield second
-        pieces_in(4)
         correlate(4)
         group(RANKS[2], WAYS[2], 4, post(4))
         yield third
-        pieces_in(6)
         correlate(6)
         group(RANKS[3], WAYS[3], 6, post(6))
 
@@ -492,7 +479,14 @@
     spawn(1, diagonal())
     run()
 
-    swap_back = send(back_a.at[other, :], recv_a, partner)
+    def code_a(i, _):
+        rows = pl.ds(pl.multiple_of(i * 32, 32), 32)
+        there = pl.ds(pl.multiple_of(i * 32 + frames, 32), 32)
+        send_a[rows, :] = encode(back_a[there, :])
+        return 0
+
+    lax.fori_loop(0, frames // 32, code_a, 0)
+    swap_back = send(send_a, recv_a, partner)
 
     scale = 1.0 / (2.0 * off_weight)
     corr_half = diag_f[c, 1, 0:1]
@@ -530,7 +524,7 @@
     def finish_a(i, _):
         rows = pl.ds(pl.multiple_of(i * 32, 32), 32)
         wide = (a_ref[rows, :].astype(f32) - center_a) * inv_a
-        back = back_a[rows, :] + recv_a[rows, :] + slope_ii * nb16[rows, :].astype(f32)
+        back = back_a[rows, :] + decode(recv_a[rows, :]) + slope_ii * nb16[rows, :].astype(f32)
         ga_ref[rows, :] = (inv_a * (back - mean_a - wide * inner_a)).astype(bf16)
         return 0
 
@@ -540,28 +534,39 @@
     extra_c[c] = sum(extra_y[i] for i in range(ny))
     share_c = send(extra_c.at[c], extra_c.at[c], partner)
 
-    def add_last(base, dst, at):
+    def add_last(base, store):
         for side, got in ((0, 4), (1, 5)):
-            cols = pl.ds(at if isinstance(at, int) else pl.multiple_of(at + side * piece, 128), piece)
-            if isinstance(at, int):
-                cols = pl.ds(side * piece, piece)
-            def body(i, _, side=side, got=got, cols=cols):
+            def body(i, _, side=side, got=got):
                 rows = pl.ds(pl.multiple_of(base + i * 64, 64), 64)
                 here = pl.ds(pl.multiple_of(i * 64, 64), 64)
-                dst[here, cols] = part_b[side, rows, :] + decode(ry[got, rows, :])
+                store(side, here, part_b[side, rows, :] + decode(ry[got, rows, :]))
                 return 0
             lax.fori_loop(0, frames // 64, body, 0)
 
+    def store_other(side, rows, value):
+        sum_b[rows, side * piece : (side + 1) * piece] = encode(value)
+
+    def store_own(side, rows, value):
+        full_b[rows, piece_of(c, side)] = value
+
     arrive(last_y)
-    add_last(frames, sum_b, 0)
-    swap_sum = [send(sum_b, full_b.at[:, own_half], partner)]
-    add_last(0, full_b, c * half)
+    add_last(frames, store_other)
+    swap_sum = [send(sum_b, recv_b, partner)]
+    add_last(0, store_own)
 
     arrive([share_c])
     mean_b = jnp.concatenate([extra_c[0, 0:1], extra_c[1, 0:1]], axis=1) + mean_a16 * slope_ii
     inner_b = jnp.concatenate([extra_c[0, 1:2], extra_c[1, 1:2]], axis=1) + cross_b * slope_ii
     loss_ref[...] = jnp.broadcast_to(extra_c[0, 2:3, :128] + extra_c[1, 2:3, :128], (8, 128))
     arrive(swap_sum)
+    there_half = pl.ds(pl.multiple_of((1 - c) * half, 128), half)
+
+    def take_b(i, _):
+        rows = pl.ds(pl.multiple_of(i * 32, 32), 32)
+        full_b[rows, there_half] = decode(recv_b[rows, :])
+        return 0
+
+    lax.fori_loop(0, frames // 32, take_b, 0)
 
     def finish_b(i, _):
         rows = pl.ds(pl.multiple_of(i * 32, 32), 32)
@@ -592,17 +597,17 @@
             vmem((both + 16, width), bf16),
             vmem((width, both), bf16),
             vmem((frames, width), bf16),
-            vmem((count, both, piece), bf16),
+            vmem((2, frames, piece), bf16),
             vmem((count, both + 16, piece), bf16),
             vmem((count, width, piece), f32),
             vmem((count, width, piece), bf16),
             vmem((both + 16, width), f32),
             vmem((count, both + 16, piece), f32),
-            vmem((frames, half), f32),
+            vmem((frames, half), bf16),
             vmem((frames, width), f32),
-            vmem((2 * nx, 2, 2, width), f32),
+            vmem((2, 2, 2, width), f32),
+            vmem((nx, 2, 2, width), f32),
             vmem((nz, 2, 2, width), f32),
-            vmem((ny, 2, half), f32),
             vmem((2, 3, 2, width), f32),
             vmem((nx, 3, 2, half), f32),
             vmem((nz, 3, 2, half), f32),
@@ -618,7 +623,9 @@
             ring = [vmem((count, rows, piece // 2), bf16)] * 2
             rings.append(ring + [vmem((n // 2 - 1, count, rows, piece), bf16)] * 2)
         scratch += rings[0] + rings[1] + rings[0] + rings[1] + [vmem((count - 2, both, piece), bf16)] * 2 + [
-            vmem((frames, width), f32),
+            vmem((frames, width), bf16),
+            vmem((frames, width), bf16),
+            vmem((frames, half), bf16),
             pltpu.SemaphoreType.DMA((256,)),
             pltpu.SemaphoreType.DMA((256,)),
         ]

time: 140 us -> 136 us (0.971)
  Pallas kernels: 135 us -> 132 us
    pallas_call x1, Pallas kernels: 135 us -> 132 us  [per_device(): pl.pallas_call(functools.partial(kernel, nx, nz, ny, float(frames * membe...]
where the time goes in v7:
time: 136 us
  Pallas kernels  132 us (97%)
  local copies, waits for them, and re-layouts  4.06 us (3%)
    pallas_call x1, Pallas kernels, per_device(): pl.pallas_call(functools.partial(kernel, nx, nz, ny, float(frames * membe...  132 us
    unnamed x4, local copies, waits for them, and re-layouts  2.87 us

profile of v7, /device:TPU:1, one launch (start us, length us, event | category | flops | bytes accessed | tf_op | source)
XLA Modules:
  0.0 136.2 jit_solution(9616416031008515038)
XLA Ops:
  0.6 131.5 %shard_map.49 = (bf16[320,1024]{1,0:T(8,128)(2,1)}, bf16[320,1024]{1,0:T(8,128)(2,1)}, f32[8,128]{1,0:T(8,128)}) custom-call(bf16[320,1024]{1,0:T(8,128)(2,1)} %a_ref.1, bf16[320,1024]{1,0:T(8,128)(2,1)} %b_ref.1), custom_call_target="tpu_custom_call" | custom-call | flops 8053063680 | bytes 2621440 | tf_op jit(solution)/shard_map/pallas_call | solution.py:632
  132.2 1.2 slice.3
  133.3 0.0 copy-start
  133.4 2.0 %copy.7 = bf16[320,1024]{1,0:T(8,128)(2,1)} copy(bf16[320,1024]{1,0:T(8,128)(2,1)} %get-tuple-element.12) | data formatting | bytes 1310720
  135.4 0.0 copy-done
  135.4 0.8 copy.8
Async XLA Ops:
  133.3 2.0 %copy-start = (bf16[320,1024]{1,0:T(8,128)(2,1)S(1)}, bf16[320,1024]{1,0:T(8,128)(2,1)}, u32[]{:S(2)}) copy-start(bf16[320,1024]{1,0:T(8,128)(2,1)} %get-tuple-element.13) | copy-start | bytes 1966084

commit v8 on v7

--- a/solution.py
+++ b/solution.py
@@ -67,7 +67,7 @@
     for peer in everyone:
         pl.semaphore_signal(barrier, inc=1, device_id=peer, device_id_type=MESH)
 
-    started, waited, due, clock, free = [], [], {}, [0.0], {}
+    started, due, clock, free = [], {}, [0.0], {}
 
     def work(t):
         clock[0] += t
@@ -99,8 +99,7 @@
     def arrive(copies):
         for copy in copies:
             clock[0] = max(clock[0], due[id(copy)])
-            copy.wait()
-            waited.append(id(copy))
+            copy.wait_recv()
 
     def spread_to(buf, mine, peers):
         return [send(buf.at[mine], buf.at[mine], peer) for peer in peers]
@@ -476,7 +475,7 @@
     for entry in live:
         entry[3] = next(entry[2])
     spawn(0, blocks())
-    spawn(1, diagonal())
+    spawn(2, diagonal())
     run()
 
     def code_a(i, _):
@@ -576,7 +575,8 @@
         return 0
 
     lax.fori_loop(0, frames // 32, finish_b, 0)
-    arrive([copy for copy in started if id(copy) not in waited])
+    for copy in started:
+        copy.wait_send()
 
 
 def solution(mesh):

time: 136 us -> 138 us (1.015)
    pallas_call x1, Pallas kernels: 132 us -> 133 us  [per_device(): pl.pallas_call(functools.partial(kernel, nx, nz, ny, float(frames * membe...]
where the time goes in v8:
time: 138 us
  Pallas kernels  133 us (96%)
  local copies, waits for them, and re-layouts  4.06 us (3%)
    pallas_call x1, Pallas kernels, per_device(): pl.pallas_call(functools.partial(kernel, nx, nz, ny, float(frames * membe...  133 us
    unnamed x4, local copies, waits for them, and re-layouts  2.87 us

profile of v8, /device:TPU:1, one launch (start us, length us, event | category | flops | bytes accessed | tf_op | source)
XLA Modules:
  0.0 138.1 jit_solution(13580623285659391675)
XLA Ops:
  0.6 133.4 %shard_map.49 = (bf16[320,1024]{1,0:T(8,128)(2,1)}, bf16[320,1024]{1,0:T(8,128)(2,1)}, f32[8,128]{1,0:T(8,128)}) custom-call(bf16[320,1024]{1,0:T(8,128)(2,1)} %a_ref.1, bf16[320,1024]{1,0:T(8,128)(2,1)} %b_ref.1), custom_call_target="tpu_custom_call" | custom-call | flops 8053063680 | bytes 2621440 | tf_op jit(solution)/shard_map/pallas_call | solution.py:632
  134.0 1.2 slice.3
  135.2 0.0 copy-start
  135.2 2.0 %copy.7 = bf16[320,1024]{1,0:T(8,128)(2,1)} copy(bf16[320,1024]{1,0:T(8,128)(2,1)} %get-tuple-element.12) | data formatting | bytes 1310720
  137.2 0.0 copy-done
  137.2 0.8 copy.8
Async XLA Ops:
  135.2 2.0 %copy-start = (bf16[320,1024]{1,0:T(8,128)(2,1)S(1)}, bf16[320,1024]{1,0:T(8,128)(2,1)}, u32[]{:S(2)}) copy-start(bf16[320,1024]{1,0:T(8,128)(2,1)} %get-tuple-element.13) | copy-start | bytes 1966084

commit v9 on v4

--- a/solution.py
+++ b/solution.py
@@ -22,17 +22,13 @@
 
 
 def encode(v):
-    q = v * v
-    q = q * q
-    return jnp.where(v < 0.0, -q, q).astype(bf16)
+    return ((v * v) * (v * jnp.abs(v))).astype(bf16)
 
 
 def decode(y):
     y = y.astype(f32)
-    q = jnp.abs(y)
-    q = q * lax.rsqrt(jnp.maximum(q, tiny))
-    q = q * lax.rsqrt(jnp.maximum(q, tiny))
-    return jnp.where(y < 0.0, -q, q)
+    y = y * lax.rsqrt(jnp.maximum(jnp.abs(y), tiny))
+    return y * lax.rsqrt(jnp.maximum(jnp.abs(y), tiny))
 
 
 def kernel(
@@ -367,10 +363,9 @@
             pieces = 2 // len(ways)
             spawn(rank, chain(way, (first + at * pieces, pieces, 0, piece)))
 
-    def to_b(first):
-        work(1.5)
-        for p in (first, first + 1):
-            part_b[p] = jnp.dot(na[...], slope[p], preferred_element_type=f32)
+    def to_b(p):
+        work(0.75)
+        part_b[p] = jnp.dot(na[...], slope[p], preferred_element_type=f32)
 
     begun = []
 
@@ -422,12 +417,12 @@
     done, last_y = [], []
 
     def post(first):
-        to_b(first)
         if first:
             copies = []
             if first == 6:
                 yield lambda: "far" in done
             for p, peer, link in ((first, up, "y+"), (first + 1, down, "y-")):
+                to_b(p)
                 code(p - 2, p, p - 4 if first == 6 else None)
                 copies.append(send(sy.at[p - 2], ry.at[p - 2], peer, link))
             if first == 6:
@@ -436,6 +431,8 @@
                 spawn(0, after_y(first, copies))
             yield []
         else:
+            to_b(0)
+            to_b(1)
             done.append("own")
         to_a(first)
         squares(first)
@@ -472,8 +469,10 @@
         nat[cols, :] = jnp.transpose(na[:both, cols].astype(f32)).astype(bf16)
     work(2.0)
     correlate(0)
+    group(RANKS[0], WAYS[0], 0, post(0))
+    for entry in live:
+        entry[3] = next(entry[2])
     spawn(0, blocks())
-    group(RANKS[0], WAYS[0], 0, post(0))
     spawn(2, diagonal())
     run()
 

time: 133 us -> 137 us (1.030)
  Pallas kernels: 128 us -> 132 us
    pallas_call x1, Pallas kernels: 128 us -> 132 us  [per_device(): pl.pallas_call(functools.partial(kernel, nx, nz, ny, float(frames * membe...]
where the time goes in v9:
time: 137 us
  Pallas kernels  132 us (96%)
  local copies, waits for them, and re-layouts  4.06 us (3%)
    pallas_call x1, Pallas kernels, per_device(): pl.pallas_call(functools.partial(kernel, nx, nz, ny, float(frames * membe...  132 us
    unnamed x4, local copies, waits for them, and re-layouts  2.87 us

profile of v9, /device:TPU:1, one launch (start us, length us, event | category | flops | bytes accessed | tf_op | source)
XLA Modules:
  0.0 136.6 jit_solution(14151999984003145088)
XLA Ops:
  0.6 131.9 %shard_map.49 = (bf16[320,1024]{1,0:T(8,128)(2,1)}, bf16[320,1024]{1,0:T(8,128)(2,1)}, f32[8,128]{1,0:T(8,128)}) custom-call(bf16[320,1024]{1,0:T(8,128)(2,1)} %a_ref.1, bf16[320,1024]{1,0:T(8,128)(2,1)} %b_ref.1), custom_call_target="tpu_custom_call" | custom-call | flops 8053063680 | bytes 2621440 | tf_op jit(solution)/shard_map/pallas_call | solution.py:608
  132.5 1.2 slice.3
  133.7 0.0 copy-start
  133.7 2.0 %copy.7 = bf16[320,1024]{1,0:T(8,128)(2,1)} copy(bf16[320,1024]{1,0:T(8,128)(2,1)} %get-tuple-element.12) | data formatting | bytes 1310720
  135.7 0.0 copy-done
  135.7 0.8 copy.8
Async XLA Ops:
  133.7 2.0 %copy-start = (bf16[320,1024]{1,0:T(8,128)(2,1)S(1)}, bf16[320,1024]{1,0:T(8,128)(2,1)}, u32[]{:S(2)}) copy-start(bf16[320,1024]{1,0:T(8,128)(2,1)} %get-tuple-element.13) | copy-start | bytes 1966084

commit v10 on v4

--- a/solution.py
+++ b/solution.py
@@ -22,17 +22,13 @@
 
 
 def encode(v):
-    q = v * v
-    q = q * q
-    return jnp.where(v < 0.0, -q, q).astype(bf16)
+    return ((v * v) * (v * jnp.abs(v))).astype(bf16)
 
 
 def decode(y):
     y = y.astype(f32)
-    q = jnp.abs(y)
-    q = q * lax.rsqrt(jnp.maximum(q, tiny))
-    q = q * lax.rsqrt(jnp.maximum(q, tiny))
-    return jnp.where(y < 0.0, -q, q)
+    y = y * lax.rsqrt(jnp.maximum(jnp.abs(y), tiny))
+    return y * lax.rsqrt(jnp.maximum(jnp.abs(y), tiny))
 
 
 def kernel(
@@ -537,6 +533,12 @@
                 return 0
             lax.fori_loop(0, frames // 64, body, 0)
 
+    late = last_y + [swap_back, share_a, share_c] + share_y
+    late = [id(copy) for copy in late]
+    for copy in started:
+        if id(copy) not in late:
+            copy.wait_send()
+    before = len(started)
     arrive(last_y)
     add_last(frames, sum_b, 0)
     swap_sum = [send(sum_b, full_b.at[:, own_half], partner)]
@@ -556,8 +558,9 @@
         return 0
 
     lax.fori_loop(0, frames // 32, finish_b, 0)
-    for copy in started:
-        copy.wait_send()
+    for at, copy in enumerate(started):
+        if at >= before or id(copy) in late:
+            copy.wait_send()
 
 
 def solution(mesh):

time: 133 us -> 132 us (level)
  no operation moved by 1% of the time
where the time goes in v10:
time: 132 us
  Pallas kernels  127 us (96%)
  local copies, waits for them, and re-layouts  4.06 us (3%)
    pallas_call x1, Pallas kernels, per_device(): pl.pallas_call(functools.partial(kernel, nx, nz, ny, float(frames * membe...  127 us
    unnamed x4, local copies, waits for them, and re-layouts  2.87 us

profile of v10, /device:TPU:1, one launch (start us, length us, event | category | flops | bytes accessed | tf_op | source)
XLA Modules:
  0.0 132.0 jit_solution(11713735369839799774)
XLA Ops:
  0.6 127.3 %shard_map.49 = (bf16[320,1024]{1,0:T(8,128)(2,1)}, bf16[320,1024]{1,0:T(8,128)(2,1)}, f32[8,128]{1,0:T(8,128)}) custom-call(bf16[320,1024]{1,0:T(8,128)(2,1)} %a_ref.1, bf16[320,1024]{1,0:T(8,128)(2,1)} %b_ref.1), custom_call_target="tpu_custom_call" | custom-call | flops 8053063680 | bytes 2621440 | tf_op jit(solution)/shard_map/pallas_call | solution.py:612
  128.0 1.2 slice.3
  129.2 0.0 copy-start
  129.2 2.0 %copy.7 = bf16[320,1024]{1,0:T(8,128)(2,1)} copy(bf16[320,1024]{1,0:T(8,128)(2,1)} %get-tuple-element.12) | data formatting | bytes 1310720
  131.2 0.0 copy-done
  131.2 0.8 copy.8
Async XLA Ops:
  129.2 2.0 %copy-start = (bf16[320,1024]{1,0:T(8,128)(2,1)S(1)}, bf16[320,1024]{1,0:T(8,128)(2,1)}, u32[]{:S(2)}) copy-start(bf16[320,1024]{1,0:T(8,128)(2,1)} %get-tuple-element.13) | copy-start | bytes 1966084

commit v11 on v10

--- a/solution.py
+++ b/solution.py
@@ -425,10 +425,12 @@
                 yield lambda: "far" in done
             for p, peer, link in ((first, up, "y+"), (first + 1, down, "y-")):
                 code(p - 2, p, p - 4 if first == 6 else None)
-                copies.append(send(sy.at[p - 2], ry.at[p - 2], peer, link))
-            if first == 6:
-                last_y.extend(copies)
-            else:
+                if first == 6:
+                    last_y.extend(
+                        send(sy.at[p - 2, rows], ry.at[p - 2, rows], peer, link) for rows in (other, own))
+                else:
+                    copies.append(send(sy.at[p - 2], ry.at[p - 2], peer, link))
+            if first < 6:
                 spawn(0, after_y(first, copies))
             yield []
         else:
@@ -539,9 +541,10 @@
         if id(copy) not in late:
             copy.wait_send()
     before = len(started)
-    arrive(last_y)
+    arrive(last_y[0::2])
     add_last(frames, sum_b, 0)
     swap_sum = [send(sum_b, full_b.at[:, own_half], partner)]
+    arrive(last_y[1::2])
     add_last(0, full_b, c * half)
 
     arrive([share_c])

time: 132 us -> 132 us (level)
  no operation moved by 1% of the time
where the time goes in v11:
time: 132 us
  Pallas kernels  127 us (96%)
  local copies, waits for them, and re-layouts  4.06 us (3%)
    pallas_call x1, Pallas kernels, per_device(): pl.pallas_call(functools.partial(kernel, nx, nz, ny, float(frames * membe...  127 us
    unnamed x4, local copies, waits for them, and re-layouts  2.87 us

profile of v11, /device:TPU:1, one launch (start us, length us, event | category | flops | bytes accessed | tf_op | source)
XLA Modules:
  0.0 132.0 jit_solution(8571099674304629979)
XLA Ops:
  0.6 127.3 %shard_map.49 = (bf16[320,1024]{1,0:T(8,128)(2,1)}, bf16[320,1024]{1,0:T(8,128)(2,1)}, f32[8,128]{1,0:T(8,128)}) custom-call(bf16[320,1024]{1,0:T(8,128)(2,1)} %a_ref.1, bf16[320,1024]{1,0:T(8,128)(2,1)} %b_ref.1), custom_call_target="tpu_custom_call" | custom-call | flops 8053063680 | bytes 2621440 | tf_op jit(solution)/shard_map/pallas_call | solution.py:615
  128.0 1.2 slice.3
  129.2 0.0 copy-start
  129.2 2.0 %copy.7 = bf16[320,1024]{1,0:T(8,128)(2,1)} copy(bf16[320,1024]{1,0:T(8,128)(2,1)} %get-tuple-element.12) | data formatting | bytes 1310720
  131.2 0.0 copy-done
  131.2 0.8 copy.8
Async XLA Ops:
  129.2 2.0 %copy-start = (bf16[320,1024]{1,0:T(8,128)(2,1)S(1)}, bf16[320,1024]{1,0:T(8,128)(2,1)}, u32[]{:S(2)}) copy-start(bf16[320,1024]{1,0:T(8,128)(2,1)} %get-tuple-element.13) | copy-start | bytes 1966084

commit v12 on v11

--- a/solution.py
+++ b/solution.py
@@ -460,7 +460,7 @@
         correlate(6)
         group(RANKS[3], WAYS[3], 6, post(6))
 
-    WAYS = [[one_way], [one_way], [other_way], [one_way]]
+    WAYS = [[one_way, other_way], [one_way], [other_way], [one_way]]
     RANKS = [4, 3, 2, 1]
 
     row_acc[...] = jnp.zeros_like(row_acc)

time: 132 us -> 137 us (1.038)
  Pallas kernels: 127 us -> 132 us
    pallas_call x1, Pallas kernels: 127 us -> 132 us  [per_device(): pl.pallas_call(functools.partial(kernel, nx, nz, ny, float(frames * membe...]
where the time goes in v12:
time: 137 us
  Pallas kernels  132 us (96%)
  local copies, waits for them, and re-layouts  4.06 us (3%)
    pallas_call x1, Pallas kernels, per_device(): pl.pallas_call(functools.partial(kernel, nx, nz, ny, float(frames * membe...  132 us
    unnamed x4, local copies, waits for them, and re-layouts  2.87 us

profile of v12, /device:TPU:1, one launch (start us, length us, event | category | flops | bytes accessed | tf_op | source)
XLA Modules:
  0.0 137.1 jit_solution(7808707333502670148)
XLA Ops:
  0.6 132.4 %shard_map.49 = (bf16[320,1024]{1,0:T(8,128)(2,1)}, bf16[320,1024]{1,0:T(8,128)(2,1)}, f32[8,128]{1,0:T(8,128)}) custom-call(bf16[320,1024]{1,0:T(8,128)(2,1)} %a_ref.1, bf16[320,1024]{1,0:T(8,128)(2,1)} %b_ref.1), custom_call_target="tpu_custom_call" | custom-call | flops 8053063680 | bytes 2621440 | tf_op jit(solution)/shard_map/pallas_call | solution.py:615
  133.0 1.2 slice.3
  134.2 0.0 copy-start
  134.2 2.0 %copy.7 = bf16[320,1024]{1,0:T(8,128)(2,1)} copy(bf16[320,1024]{1,0:T(8,128)(2,1)} %get-tuple-element.12) | data formatting | bytes 1310720
  136.2 0.0 copy-done
  136.2 0.8 copy.8
Async XLA Ops:
  134.2 2.0 %copy-start = (bf16[320,1024]{1,0:T(8,128)(2,1)S(1)}, bf16[320,1024]{1,0:T(8,128)(2,1)}, u32[]{:S(2)}) copy-start(bf16[320,1024]{1,0:T(8,128)(2,1)} %get-tuple-element.13) | copy-start | bytes 1966084
